TPU v7x, 32 devices: a whole 2x2x4 slice. The times are simulated.
32 devices in a mesh: vert: 8 (over z, y), edge: 4 (over x, core).
Axes of the slice: x: 2, y: 2, z: 4, core: 2. Of those that a mesh axis runs over, the one named last changes fastest.
Arguments:
- features: float32 [16384, 256], P('vert'), may hold values from -6 to 6
- incidence: bfloat16 [64, 128, 512], P('vert', None, 'edge'), may hold values from 0 to 1, as said below
- send_count: int32 [64, 4], P('vert', 'edge'), may hold values from 0 to 1, as said below
- row_block: int32 [64, 4], P('vert', 'edge'), may hold values from 0 to 15
- edge_block: int32 [64, 4], P('vert', 'edge'), may hold values from 0 to 1
- edge_weight: float32 [16, 512], P('vert', 'edge'), may hold values from 0.25 to 4
- edge_degree: int32 [16, 512], P('vert', 'edge'), may hold values from 0 to 1024, as said below
- vertex_degree: int32 [16384], P('vert'), may hold values from 0 to 4096, as said below
Outputs:
- smoothed: float32 [16384, 256], P(('vert', 'edge'))
Inputs may be any that keep to these rules, and one draw needn't show every extreme that they name: `incidence`: tile entries are 0 or 1. `send_count`: for each edge index one hyperedge block receives a live tile from every index of vert, in every draw. `edge_degree`: the column sums of H over live tiles; the most is reached in every draw. `vertex_degree`: the row sums of H over live tiles; the most is reached in every draw.
All inputs are finite; a program needn't handle non-finite values.
Results may differ from a plain program's by a relative error of at most 0.0049.
Values may be sent and summed in bfloat16 or wider, within the bound.
A program may use at most 64 MiB of HBM per device.

v0:
```python
import jax
import jax.numpy as jnp
from jax import lax
from jax.sharding import PartitionSpec as P


def shards(
    features, incidence, send_count, row_block, edge_block, edge_weight, edge_degree, vertex_degree
):
    vert_total = lax.axis_size("vert")
    edge_total = lax.axis_size("edge")
    paper_rows = features.shape[0]
    width = features.shape[1]
    tile_rows = incidence.shape[1]
    block_count = paper_rows // tile_rows
    hyper_blocks = edge_weight.shape[0]
    share = paper_rows // edge_total
    live_slot = send_count[:, 0].astype(jnp.float32)
    row_index = row_block[:, 0]
    edge_index = edge_block[:, 0]
    row_scale = (1.0 / jnp.sqrt(jnp.maximum(vertex_degree, 1).astype(jnp.float32)))[:, None]
    hyper_scale = (edge_weight / jnp.maximum(edge_degree, 1).astype(jnp.float32))[:, :, None]
    row_choose = (row_index[None, :] == jnp.arange(block_count)[:, None]).astype(
        jnp.float32
    ) * live_slot[None, :]
    hyper_ids = jnp.arange(hyper_blocks)
    scaled = (row_scale * features).astype(jnp.bfloat16)
    result = None
    for applied in range(2):
        picked = scaled.reshape(block_count, tile_rows, width)[row_index]
        partial_value = jnp.einsum(
            "spq,spf->sqf", incidence, picked, preferred_element_type=jnp.float32
        )
        partial_value = (partial_value * live_slot[:, None, None]).astype(jnp.bfloat16)
        arrived = lax.all_to_all(partial_value, "vert", split_axis=0, concat_axis=0, tiled=True)
        arrived_block = lax.all_to_all(edge_index, "vert", split_axis=0, concat_axis=0, tiled=True)
        select = (arrived_block[None, :] == hyper_ids[:, None]).astype(jnp.bfloat16)
        summed = jnp.dot(
            select,
            arrived.reshape(vert_total, tile_rows * width),
            preferred_element_type=jnp.float32,
        )
        hyper_feat = (summed.reshape(hyper_blocks, tile_rows, width) * hyper_scale).astype(
            jnp.bfloat16
        )
        answer = hyper_feat[arrived_block]
        returned = lax.all_to_all(answer, "vert", split_axis=0, concat_axis=0, tiled=True)
        spread = jnp.einsum("spq,sqf->spf", incidence, returned, preferred_element_type=jnp.float32)
        rows_out = jnp.dot(
            row_choose,
            spread.reshape(vert_total, tile_rows * width),
            precision=lax.Precision.HIGHEST,
            preferred_element_type=jnp.float32,
        )
        partial_rows = rows_out.reshape(paper_rows, width)
        own_sum = lax.psum_scatter(partial_rows, "edge", scatter_dimension=0, tiled=True)
        own_scale = lax.dynamic_slice_in_dim(row_scale, lax.axis_index("edge") * share, share, 0)
        current = own_scale * own_sum
        if applied == 0:
            scaled = lax.all_gather(
                (own_scale * current).astype(jnp.bfloat16), "edge", axis=0, tiled=True
            )
        else:
            result = current
    return result


def solution(mesh):
    placed = (
        P("vert", None),
        P("vert", None, "edge"),
        P("vert", "edge"),
        P("vert", "edge"),
        P("vert", "edge"),
        P("vert", "edge"),
        P("vert", "edge"),
        P("vert"),
    )
    return jax.shard_map(
        shards, mesh=mesh, in_specs=placed, out_specs=P(("vert", "edge"), None), check_vma=False
    )
```

profile of v0, /device:TPU:0, one launch (start us, length us, event | category | flops | bytes accessed | tf_op | source)
XLA Modules:
  0.0 198.6 jit_solution(10071457186867197186)
XLA Ops:
  6.5 1.4 copy.29
  7.9 7.3 %all-to-all-start = ((s32[8,1,1]{2,1,0:T(1,128)}), s32[8,1,1]{2,1,0:T(1,128)S(1)}, u32[]{:S(2)}, u32[]{:S(2)}) async-start(s32[8,1,1]{2,1,0:T(1,128)} %copy.29), calls=%async_computation | async-start | bytes 8192 | tf_op jit(solution)/shard_map/all_to_all | solution.py:36
  15.2 0.7 convert_bitcast_fusion
  15.8 0.7 fusion.18
  16.5 0.7 convert_rsqrt_fusion
  17.2 1.9 multiply_convert_fusion
  19.2 0.6 gather_fusion
  19.8 1.1 fusion.3
  20.9 0.7 all-to-all-done
  21.7 5.3 %all-to-all-start.1 = ((bf16[8,128,256]{1,2,0:T(8,128)(2,1)}), bf16[8,128,256]{1,2,0:T(8,128)(2,1)S(1)}, u32[]{:S(2)}, u32[]{:S(2)}) async-start(bf16[8,128,256]{1,2,0:T(8,128)(2,1)} %fusion.3), calls=%async_computation.1 | async-start | bytes 1048576 | tf_op jit(solution)/shard_map/all_to_all | solution.py:35
  26.9 0.0 reduce-scatter.3.cloned.1.call-start
  27.0 0.1 copy.32
  27.1 0.2 reduce
  27.4 13.5 %all-to-all-done.1 = bf16[8,128,256]{1,2,0:T(8,128)(2,1)S(1)} async-done(((bf16[8,128,256]{1,2,0:T(8,128)(2,1)}), bf16[8,128,256]{1,2,0:T(8,128)(2,1)S(1)}, u32[]{:S(2)}, u32[]{:S(2)}) %all-to-all-start.1) | async-done | bytes 524320 | tf_op jit(solution)/shard_map/all_to_all | solution.py:35
  40.9 0.2 copy.31
  41.1 0.4 fusion.4
  41.6 0.6 gather_fusion.1
  42.2 0.3 copy.34
  42.4 17.6 %all_to_all.33 = bf16[8,128,256]{1,2,0:T(8,128)(2,1)S(1)} all-to-all(bf16[8,128,256]{1,2,0:T(8,128)(2,1)S(1)} %copy.34), channel_id=1, replica_groups=mesh['vert'=8,'edge'=4] {'vert'}, dimensions={0} | all-to-all | bytes 1048576 | tf_op jit(solution)/shard_map/all_to_all | solution.py:47
  60.0 0.3 convolution_bitcast_fusion.1
  60.4 0.3 copy.35
  60.7 0.6 copy.44
  61.3 1.8 fusion.8
  63.1 1.5 reshape.80
  64.6 0.0 reduce-scatter.3.cloned.1.call-update
  64.7 0.0 all-gather.2.cloned.1.call-start
  64.7 0.1 dynamic-slice.3
  64.8 30.5 %reduce-scatter.3.cloned.1.call-done = f32[512,256]{1,0:T(8,128)} async-done(((f32[2048,256]{1,0:T(8,128)}), f32[512,256]{1,0:T(8,128)}) %reduce-scatter.3.cloned.1.call-update) | async-done | bytes 524304 | tf_op jit(solution)/shard_map/reduce_scatter | solution.py:56
  95.3 1.9 multiply_convert_fusion.1
  97.2 0.0 all-gather.2.cloned.1.call-update
  97.2 0.0 reduce-scatter.5.cloned.1.call-start
  97.2 16.8 %all-gather.2.cloned.1.call-done = bf16[2048,256]{1,0:T(8,128)(2,1)} async-done(((bf16[512,256]{1,0:T(8,128)(2,1)}), bf16[2048,256]{1,0:T(8,128)(2,1)}) %all-gather.2.cloned.1.call-update) | async-done | bytes 1048592 | tf_op jit(solution)/shard_map/all_gather | solution.py:60
  114.1 1.8 gather_fusion.2
  115.9 0.3 fusion.2
  116.2 20.2 %all_to_all.34 = bf16[8,128,256]{1,2,0:T(8,128)(2,1)S(1)} all-to-all(bf16[8,128,256]{1,2,0:T(8,128)(2,1)S(1)} %fusion.2), channel_id=1, replica_groups=mesh['vert'=8,'edge'=4] {'vert'}, dimensions={0} | all-to-all | bytes 1048576 | tf_op jit(solution)/shard_map/all_to_all | solution.py:35
  136.4 0.2 copy.37
  136.6 0.4 fusion.5
  137.1 0.6 gather_fusion.3
  137.7 0.3 copy.39
  138.0 17.9 %all_to_all.35 = bf16[8,128,256]{1,2,0:T(8,128)(2,1)S(1)} all-to-all(bf16[8,128,256]{1,2,0:T(8,128)(2,1)S(1)} %copy.39), channel_id=1, replica_groups=mesh['vert'=8,'edge'=4] {'vert'}, dimensions={0} | all-to-all | bytes 1048576 | tf_op jit(solution)/shard_map/all_to_all | solution.py:47
  155.9 0.3 convolution_bitcast_fusion
  156.2 0.3 copy.40
  156.5 0.6 copy.46
  157.2 1.8 fusion.6
  158.9 1.5 reshape.84
  160.5 0.0 reduce-scatter.5.cloned.1.call-update
  160.5 29.6 %reduce-scatter.5.cloned.1.call-done = f32[512,256]{1,0:T(8,128)} async-done(((f32[2048,256]{1,0:T(8,128)}), f32[512,256]{1,0:T(8,128)}) %reduce-scatter.5.cloned.1.call-update) | async-done | bytes 524304 | tf_op jit(solution)/shard_map/reduce_scatter | solution.py:56
  190.1 2.0 broadcast_multiply_fusion
  (14 shorter events, 0.1 us)
Async XLA Ops:
  6.5 13.2 %copy-start = (bf16[8,128,128]{2,1,0:T(8,128)(2,1)S(1)}, bf16[8,128,128]{2,1,0:T(8,128)(2,1)}, u32[]{:S(2)}) copy-start(bf16[8,128,128]{2,1,0:T(8,128)(2,1)} %param.9) | copy-start | bytes 786436
  7.9 13.7 %all-to-all-start = ((s32[8,1,1]{2,1,0:T(1,128)}), s32[8,1,1]{2,1,0:T(1,128)S(1)}, u32[]{:S(2)}, u32[]{:S(2)}) async-start(s32[8,1,1]{2,1,0:T(1,128)} %copy.29), calls=%async_computation | async-start | bytes 8192 | tf_op jit(solution)/shard_map/all_to_all | solution.py:36
  19.1 7.8 %copy-start.2 = (f32[2,128]{1,0:T(2,128)S(1)}, f32[2,128]{1,0:T(2,128)}, u32[]{:S(2)}) copy-start(f32[2,128]{1,0:T(2,128)} %param.13) | copy-start | bytes 3076
  19.2 7.8 %copy-start.3 = (s32[2,128]{1,0:T(2,128)S(1)}, s32[2,128]{1,0:T(2,128)}, u32[]{:S(2)}) copy-start(s32[2,128]{1,0:T(2,128)} %param.14) | copy-start | bytes 3076
  21.7 19.2 %all-to-all-start.1 = ((bf16[8,128,256]{1,2,0:T(8,128)(2,1)}), bf16[8,128,256]{1,2,0:T(8,128)(2,1)S(1)}, u32[]{:S(2)}, u32[]{:S(2)}) async-start(bf16[8,128,256]{1,2,0:T(8,128)(2,1)} %fusion.3), calls=%async_computation.1 | async-start | bytes 1048576 | tf_op jit(solution)/shard_map/all_to_all | solution.py:35
  26.9 68.4 %reduce-scatter.3.cloned.1.call-start = ((), (), s32[]{:S(2)}) async-start(), calls=%async_computation.7 | async-start | bytes 2621440 | tf_op jit(solution)/shard_map/reduce_scatter | solution.py:56
  60.4 1.0 copy-start.1
  64.7 49.4 %all-gather.2.cloned.1.call-start = ((), (), s32[]{:S(2)}) async-start(), calls=%async_computation.8 | async-start | bytes 1310720 | tf_op jit(solution)/shard_map/all_gather | solution.py:60
  97.2 92.9 %reduce-scatter.5.cloned.1.call-start = ((), (), s32[]{:S(2)}) async-start(), calls=%async_computation.9 | async-start | bytes 2621440 | tf_op jit(solution)/shard_map/reduce_scatter | solution.py:56
Sparse Core Ops, SparseCore 0:
  64.8 30.4 reduce-scatter.2
  97.3 16.7 all-gather.1
  160.6 29.4 reduce-scatter.4
where the time goes:
time: 199 us
  waiting for transfers between devices  91.3 us (46%)
  blocking collectives  55.7 us (28%)
  between operations  13.3 us (7%)
  starting transfers between devices  12.7 us (6%)
  local copies, waits for them, and re-layouts  11.1 us (6%)
  other arithmetic  8.06 us (4%)
  matrix products  6.5 us (3%)
    reduce_scatter x2, waiting for transfers between devices, shards(): lax.psum_scatter(partial_rows, 'edge', scatter_dimension=0, tiled=True)  60.1 us
    all_to_all x2, blocking collectives, shards(): lax.all_to_all(answer, 'vert', split_axis=0, concat_axis=0, tiled=True)  35.5 us
    all_to_all x1, blocking collectives, shards(): lax.all_to_all(partial_value, 'vert', split_axis=0, concat_axis=0, tiled=...  20.2 us
    all_gather x1, waiting for transfers between devices, shards(): lax.all_gather((own_scale * current).astype(jnp.bfloat16), 'edge', axis=0...  16.8 us
    all_to_all x1, waiting for transfers between devices, shards(): lax.all_to_all(partial_value, 'vert', split_axis=0, concat_axis=0, tiled=...  13.5 us
    all_to_all x1, starting transfers between devices, shards(): lax.all_to_all(edge_index, 'vert', split_axis=0, concat_axis=0, tiled=True)  7.28 us
    all_to_all x1, starting transfers between devices, shards(): lax.all_to_all(partial_value, 'vert', split_axis=0, concat_axis=0, tiled=...  5.27 us
  transfers between devices with their start and end apart: 5, of which 5 were waited for; matrix products, arithmetic and copies ran while one was open for 3% of the time, Pallas kernels for 0%

commit v1 on v0

v1 whole, which is shorter than its diff:
```python
import functools
import math

import jax
import jax.numpy as jnp
from jax import lax
from jax.experimental import pallas as pl
from jax.experimental.pallas import tpu as pltpu
from jax.sharding import PartitionSpec as P

MESH = pl.DeviceIdType.MESH
LANES = 128
BF16 = jnp.bfloat16
F32 = jnp.float32


def repeat(start, stop, body):
    if stop - start <= 8:
        for step in range(start, stop):
            body(step)
    else:

        @pl.loop(start, stop)
        def _(step):
            body(step)


def kernel(
    nv,
    ne,
    cols,
    feat,
    inc,
    live_s,
    row_s,
    edge_s,
    weight,
    degree,
    vdeg,
    out,
    tiles,
    meta_e,
    scale_e,
    meta_v,
    keys,
    owner_blocks,
    xs,
    rs,
    fwd_send,
    fwd_recv,
    bwd_send,
    bwd_recv,
    acc,
    prev,
    last,
    hyper_acc,
    hyper_feat,
    fin_send,
    fin_recv,
    meta_send_sem,
    meta_recv_sem,
    scale_send_sem,
    scale_recv_sem,
    tile_send_sem,
    tile_recv_sem,
    relay_sem,
    mv_send_sem,
    mv_recv_sem,
    fwd_send_sem,
    fwd_recv_sem,
    bwd_send_sem,
    bwd_recv_sem,
    fin_send_sem,
    fin_recv_sem,
    local_sem,
):
    v = lax.axis_index("vert")
    e = lax.axis_index("edge")
    block = inc.shape[1]
    blocks = xs.shape[0]
    hyper_blocks = weight.shape[0]
    share = blocks // ne
    none = nv * ne
    sibling = e + 1 - 2 * (e % 2)

    def edge_at(j):
        base = e + (j % 2) * (sibling - e)
        return (base + 2 * (j // 2)) % ne

    def to_edge(src, dst, send_sem, recv_sem, target):
        return pltpu.make_async_remote_copy(
            src_ref=src,
            dst_ref=dst,
            send_sem=send_sem,
            recv_sem=recv_sem,
            device_id=(v, target),
            device_id_type=MESH,
        )

    def to_vert(src, dst, send_sem, recv_sem, target):
        return pltpu.make_async_remote_copy(
            src_ref=src,
            dst_ref=dst,
            send_sem=send_sem,
            recv_sem=recv_sem,
            device_id=(target, e),
            device_id_type=MESH,
        )

    barrier = pltpu.get_barrier_semaphore()

    def greet_vert(t):
        pl.semaphore_signal(barrier, inc=1, device_id=((v + t) % nv, e), device_id_type=MESH)

    repeat(1, nv, greet_vert)
    for j in range(1, ne):
        pl.semaphore_signal(barrier, inc=1, device_id=(v, edge_at(j)), device_id_type=MESH)

    lane = lax.broadcasted_iota(jnp.int32, (8, LANES), 1)
    sub = lax.broadcasted_iota(jnp.int32, (8, LANES), 0)
    packed = jnp.zeros((8, LANES), jnp.int32)
    for s in range(nv):
        key = jnp.where(live_s[s, 0] > 0, row_s[s, 0], -1)
        both = jnp.where(sub == 0, key, edge_s[s, 0])
        packed = jnp.where(lane == s, both, packed)
    meta_e[e] = packed
    scale_e[e, :hyper_blocks] = weight[...] / jnp.maximum(degree[...], 1).astype(F32)

    pl.semaphore_wait(barrier, nv - 1 + ne - 1)

    meta_copies, tile_copies = [], []
    for j in range(1, ne):
        target = edge_at(j)
        meta_copies.append(
            to_edge(
                meta_e.at[e], meta_e.at[e], meta_send_sem.at[j], meta_recv_sem.at[e], target
            )
        )
        meta_copies.append(
            to_edge(
                scale_e.at[e], scale_e.at[e], scale_send_sem.at[j], scale_recv_sem.at[e], target
            )
        )
    for copy in meta_copies:
        copy.start()
    for j in [1] + list(range(2, ne, 2)):
        copy = to_edge(
            inc, tiles.at[e], tile_send_sem.at[j], tile_recv_sem.at[e], edge_at(j)
        )
        copy.start()
        tile_copies.append(copy)

    rs[...] = 1.0 / jnp.sqrt(jnp.maximum(vdeg[...], 1).astype(F32))
    group = LANES // cols
    start = pl.multiple_of((e // group) * LANES, LANES)
    part = e % group
    for b in range(blocks):
        turned = feat[pl.ds(b * block, block), pl.ds(start, LANES)].T
        picked = turned[:cols]
        for g in range(1, group):
            picked = jnp.where(part == g, turned[g * cols : (g + 1) * cols], picked)
        xs[b] = (picked * rs[b : b + 1, :]).astype(BF16)

    def tile_of(j, s):
        return inc[s] if j == 0 else tiles[edge_at(j), s]

    def partial(j, s):
        if j == 0:
            alive = live_s[s, 0] > 0
            row = row_s[s, 0]
        else:
            key = keys[edge_at(j), 0, s]
            alive = key >= 0
            row = jnp.maximum(key, 0)
        value = jnp.dot(xs[row], tile_of(j, s), preferred_element_type=F32)
        return jnp.where(alive, value, 0.0).astype(BF16)

    def fwd_copy(t):
        return to_vert(
            fwd_send.at[t],
            fwd_recv.at[v],
            fwd_send_sem.at[t],
            fwd_recv_sem.at[v],
            (v + t) % nv,
        )

    def fwd_arrival(source):
        return to_vert(
            fwd_send.at[0], fwd_recv.at[source], fwd_send_sem.at[0], fwd_recv_sem.at[source], v
        )

    def bwd_copy(t):
        return to_vert(
            bwd_send.at[t],
            bwd_recv.at[v],
            bwd_send_sem.at[t],
            bwd_recv_sem.at[v],
            (v + t) % nv,
        )

    def bwd_arrival(source):
        return to_vert(
            bwd_send.at[0], bwd_recv.at[source], bwd_send_sem.at[0], bwd_recv_sem.at[source], v
        )

    def mv_copy(t):
        return to_vert(
            meta_v.at[v], meta_v.at[v], mv_send_sem.at[t], mv_recv_sem.at[v], (v + t) % nv
        )

    def mv_arrival(source):
        return to_vert(
            meta_v.at[v], meta_v.at[source], mv_send_sem.at[0], mv_recv_sem.at[source], v
        )

    def tile_arrival(source):
        return to_edge(inc, tiles.at[source], tile_send_sem.at[0], tile_recv_sem.at[source], e)

    def first_part(j):
        here = edge_at(j)

        def step(t):
            fwd_send[t, here] = partial(j, (v + t) % nv)
            to_vert(
                fwd_send.at[t, here],
                fwd_recv.at[v, here],
                fwd_send_sem.at[t],
                fwd_recv_sem.at[v],
                (v + t) % nv,
            ).start()

        repeat(1, nv, step)
        fwd_recv[v, here] = partial(j, v)

    first_part(0)

    for j in range(1, ne):
        source = edge_at(j)
        to_edge(
            meta_e.at[e], meta_e.at[source], meta_send_sem.at[0], meta_recv_sem.at[source], e
        ).wait_recv()
        to_edge(
            scale_e.at[e], scale_e.at[source], scale_send_sem.at[0], scale_recv_sem.at[source], e
        ).wait_recv()
    to_scalars = pltpu.make_async_copy(meta_e, keys, local_sem.at[0])
    to_scalars.start()
    seen = jnp.zeros((8, LANES), jnp.int32)
    for other in range(ne):
        seen = jnp.where(sub == other, meta_e[other, 1:2, :], seen)
    meta_v[v] = seen
    repeat(1, nv, lambda t: mv_copy(t).start())
    to_scalars.wait()

    relays = []
    for j in range(1, ne):
        source = edge_at(j)
        tile_arrival(source).wait_recv()
        if j >= 2 and j % 2 == 0:
            copy = to_edge(
                tiles.at[source],
                tiles.at[source],
                relay_sem.at[j],
                tile_recv_sem.at[source],
                sibling,
            )
            copy.start()
            relays.append(copy)
        first_part(j)

    def link(i, latest):
        key = keys[edge_at(i % ne), 0, (v - i // ne + nv) % nv]
        before = none
        for b in range(blocks):
            before = jnp.where(key == b, latest[b], before)
        prev[i] = before
        return tuple(jnp.where(key == b, i, latest[b]) for b in range(blocks))

    latest = lax.fori_loop(0, none, link, (jnp.int32(none),) * blocks)
    for b in range(blocks):
        last[b] = latest[b]
    acc[none] = jnp.zeros(acc.shape[1:], F32)

    repeat(1, nv, lambda t: mv_arrival((v - t + nv) % nv).wait_recv())
    to_scalars = pltpu.make_async_copy(meta_v, owner_blocks, local_sem.at[1])
    to_scalars.start()
    to_scalars.wait()

    for applied in range(2):
        if applied:

            def send_all(t):
                for j in range(ne):
                    fwd_send[t, edge_at(j)] = partial(j, (v + t) % nv)
                fwd_copy(t).start()

            repeat(1, nv, send_all)
            for j in range(ne):
                fwd_recv[v, edge_at(j)] = partial(j, v)

        def add_from(source, first):
            for other in range(ne):
                held = owner_blocks[source, other, v]
                value = fwd_recv[source, other].astype(F32)
                for h in range(hyper_blocks):
                    term = jnp.where(held == h, value, 0.0)
                    hyper_acc[h, other] = term if first else hyper_acc[h, other] + term

        add_from(v, True)

        def arrive(t):
            source = (v - t + nv) % nv
            fwd_arrival(source).wait_recv()
            add_from(source, False)

        repeat(1, nv, arrive)
        for other in range(ne):
            for h in range(hyper_blocks):
                hyper_feat[h, other] = (
                    hyper_acc[h, other] * scale_e[other, h : h + 1, :]
                ).astype(BF16)

        def answer(t):
            if applied:
                bwd_copy(t).wait_send()
            for other in range(ne):
                held = owner_blocks[(v + t) % nv, other, v]
                bwd_send[t, other] = hyper_feat[held, other]
            bwd_copy(t).start()

        repeat(1, nv, answer)
        for other in range(ne):
            bwd_recv[v, other] = hyper_feat[owner_blocks[v, other, v], other]
        repeat(1, nv, lambda t: fwd_copy(t).wait_send())

        def spread(t):
            slot = (v - t + nv) % nv
            for j in range(ne):
                i = t * ne + j
                value = lax.dot_general(
                    bwd_recv[slot, edge_at(j)],
                    tile_of(j, slot),
                    (((1,), (1,)), ((), ())),
                    preferred_element_type=F32,
                )
                acc[i] = value + acc[prev[i]]

        spread(0)

        def come_back(t):
            bwd_arrival((v - t + nv) % nv).wait_recv()
            spread(t)

        repeat(1, nv, come_back)

        if applied == 0:
            for b in range(blocks):
                scale = rs[b : b + 1, :]
                xs[b] = (scale * (scale * acc[last[b]])).astype(BF16)

    fin_copies = []
    for j in range(ne - 1, -1, -1):
        target = edge_at(j)
        for k in range(share):
            b = target * share + k
            value = (rs[pl.ds(b, 1), :] * acc[last[b]]).astype(BF16)
            if j:
                fin_send[j, k] = value
            else:
                fin_recv[e, k] = value
        if j:
            copy = to_edge(
                fin_send.at[j], fin_recv.at[e], fin_send_sem.at[j], fin_recv_sem.at[e], target
            )
            copy.start()
            fin_copies.append(copy)
    for j in range(1, ne):
        source = edge_at(j)
        to_edge(
            fin_send.at[0], fin_recv.at[source], fin_send_sem.at[0], fin_recv_sem.at[source], e
        ).wait_recv()
    for k in range(share):
        for g in range(ne // group):
            stacked = jnp.concatenate(
                [fin_recv[g * group + i, k].astype(F32) for i in range(group)], axis=0
            )
            out[pl.ds(k * block, block), pl.ds(g * LANES, LANES)] = stacked.T

    for copy in meta_copies + tile_copies + relays + fin_copies:
        copy.wait_send()
    repeat(1, nv, lambda t: mv_copy(t).wait_send())
    repeat(1, nv, lambda t: bwd_copy(t).wait_send())


def shards(
    features, incidence, send_count, row_block, edge_block, edge_weight, edge_degree, vertex_degree
):
    nv = lax.axis_size("vert")
    ne = lax.axis_size("edge")
    papers, width = features.shape
    slots, block, _ = incidence.shape
    blocks = papers // block
    hyper_blocks = edge_weight.shape[0]
    cols = width // ne
    share = blocks // ne
    scratch = [
        ((ne, slots, block, block), BF16),
        ((ne, 8, LANES), jnp.int32),
        ((ne, 8, LANES), F32),
        ((nv, 8, LANES), jnp.int32),
        None,
        None,
        ((blocks, cols, block), BF16),
        ((blocks, block), F32),
        ((nv, ne, cols, block), BF16),
        ((nv, ne, cols, block), BF16),
        ((nv, ne, cols, block), BF16),
        ((nv, ne, cols, block), BF16),
        ((nv * ne + 1, cols, block), F32),
        None,
        None,
        ((hyper_blocks, ne, cols, block), F32),
        ((hyper_blocks, ne, cols, block), BF16),
        ((ne, share, cols, block), BF16),
        ((ne, share, cols, block), BF16),
    ]
    scalars = iter(
        [(ne, 8, LANES), (nv, 8, LANES), (nv * ne,), (blocks,)]
    )
    held = sum(
        math.prod(item[0]) * jnp.dtype(item[1]).itemsize for item in scratch if item is not None
    )
    held += features.size * 4 + incidence.size * 2 + papers // ne * width * 4
    shapes = [
        pltpu.SMEM(next(scalars), jnp.int32) if item is None else pltpu.VMEM(*item)
        for item in scratch
    ]
    dma = pltpu.SemaphoreType.DMA
    sems = [dma((ne,))] * 7 + [dma((nv,))] * 6 + [dma((ne,))] * 2 + [dma((2,))]
    vmem = pl.BlockSpec(memory_space=pltpu.VMEM)
    smem = pl.BlockSpec(memory_space=pltpu.SMEM)
    return pl.pallas_call(
        functools.partial(kernel, nv, ne, cols),
        out_shape=jax.ShapeDtypeStruct((papers // ne, width), F32),
        in_specs=[vmem, vmem, smem, smem, smem, vmem, vmem, vmem],
        out_specs=vmem,
        scratch_shapes=shapes + sems,
        compiler_params=pltpu.CompilerParams(
            collective_id=0,
            has_side_effects=True,
            vmem_limit_bytes=held + 6 * 2**20,
        ),
        cost_estimate=pl.CostEstimate(
            flops=8 * slots * ne * block * block * cols,
            bytes_accessed=features.size * 4 + incidence.size * 2,
            transcendentals=0,
        ),
    )(
        features,
        incidence,
        send_count,
        row_block,
        edge_block,
        edge_weight,
        edge_degree,
        vertex_degree.reshape(blocks, block),
    )


def solution(mesh):
    placed = (
        P("vert", None),
        P("vert", None, "edge"),
        P("vert", "edge"),
        P("vert", "edge"),
        P("vert", "edge"),
        P("vert", "edge"),
        P("vert", "edge"),
        P("vert"),
    )
    return jax.shard_map(
        shards, mesh=mesh, in_specs=placed, out_specs=P(("vert", "edge"), None), check_vma=False
    )
```

time: 199 us -> 71.6 us (0.36)
  waiting for transfers between devices: 91.3 us -> 0 us
  Pallas kernels: 0 us -> 63.8 us
  blocking collectives: 55.7 us -> 0 us
  between operations: 13.3 us -> 0.02 us
  starting transfers between devices: 12.7 us -> 0 us
  other arithmetic: 8.06 us -> 0 us
  matrix products: 6.5 us -> 0 us
  local copies, waits for them, and re-layouts: 11.1 us -> 7.58 us
    pallas_call x0 -> x1, Pallas kernels: none -> 63.8 us  [shards(): pl.pallas_call(functools.partial(kernel, nv, ne, cols), out_shape=jax.Sha...]
    reduce_scatter x2 -> x0, waiting for transfers between devices: 60.1 us -> none  [shards(): lax.psum_scatter(partial_rows, 'edge', scatter_dimension=0, tiled=True)]
    all_to_all x3 -> x0, blocking collectives: 55.7 us -> none  [the longest x2 35.5 us: shards(): lax.all_to_all(answer, 'vert', split_axis=0, concat_axis=0, tiled=True)]
    all_gather x1 -> x0, waiting for transfers between devices: 16.8 us -> none  [shards(): lax.all_gather((own_scale * current).astype(jnp.bfloat16), 'edge', axis=0...]
    all_to_all x2 -> x0, waiting for transfers between devices: 14.3 us -> none  [the longest x1 13.5 us: shards(): lax.all_to_all(partial_value, 'vert', split_axis=0, concat_axis=0, tiled=...]
    all_to_all x2 -> x0, starting transfers between devices: 12.5 us -> none  [the longest x1 7.28 us: shards(): lax.all_to_all(edge_index, 'vert', split_axis=0, concat_axis=0, tiled=True)]
    dot_general x8 -> x0, matrix products: 6.5 us -> none  [the longest x2 3.54 us: shards(): jnp.dot(row_choose, spread.reshape(vert_total, tile_rows * width), precis...]
    unnamed x10 -> x14, local copies, waits for them, and re-layouts: 1.25 us -> 7.58 us
  transfers between devices with their start and end apart: 5 -> 0, of which waited for: 5 -> 0; matrix products, arithmetic and copies ran while one was open for 3% -> 0% of each run, Pallas kernels for 0% -> 0%
where the time goes in v1:
time: 71.6 us; the launch traced here: 71.3 us
  Pallas kernels  63.8 us (89%)
  local copies, waits for them, and re-layouts  7.58 us (11%)
    pallas_call x1, Pallas kernels, shards(): pl.pallas_call(functools.partial(kernel, nv, ne, cols), out_shape=jax.Sha...  63.8 us
    unnamed x14, local copies, waits for them, and re-layouts  7.58 us

profile of v1, /device:TPU:0, one launch (start us, length us, event | category | flops | bytes accessed | tf_op | source)
XLA Modules:
  0.0 71.3 jit_solution(3483275689609628148)
XLA Ops:
  0.0 0.7 %copy.9.live_s = s32[8,1]{1,0:T(8,128)S(1)} copy(s32[8,1]{0,1:T(1,128)} %param.10) | data formatting | bytes 64 | tf_op args[2]
  0.7 0.7 %copy.10.row_s = s32[8,1]{1,0:T(8,128)S(1)} copy(s32[8,1]{0,1:T(1,128)} %param.11) | data formatting | bytes 64 | tf_op args[3]
  1.5 0.7 %copy.11.edge_s = s32[8,1]{1,0:T(8,128)S(1)} copy(s32[8,1]{0,1:T(1,128)} %param.12) | data formatting | bytes 64 | tf_op args[4]
  2.2 0.0 copy-start
  2.2 1.6 %copy-done = f32[2048,256]{1,0:T(8,128)S(1)} copy-done((f32[2048,256]{1,0:T(8,128)S(1)}, f32[2048,256]{1,0:T(8,128)}, u32[]{:S(2)}) %copy-start) | copy-done | bytes 2097176
  3.8 0.0 copy-start.1
  3.8 0.9 %copy-done.1 = bf16[8,128,128]{2,1,0:T(8,128)(2,1)S(1)} copy-done((bf16[8,128,128]{2,1,0:T(8,128)(2,1)S(1)}, bf16[8,128,128]{2,1,0:T(8,128)(2,1)}, u32[]{:S(2)}) %copy-start.1) | copy-done | bytes 262168
  4.7 0.0 copy-start.2
  4.7 0.7 copy-done.2
  5.4 0.0 copy-start.3
  5.4 0.7 copy-done.3
  6.1 0.0 copy-start.4
  6.1 0.7 copy-done.4
  6.8 63.8 %shard_map.82 = f32[512,256]{1,0:T(8,128)S(1)} custom-call(f32[2048,256]{1,0:T(8,128)S(1)} %copy-done, bf16[8,128,128]{2,1,0:T(8,128)(2,1)S(1)} %copy-done.1, s32[8,1]{1,0:T(8,128)S(1)} %copy.9.live_s, s32[8,1]{1,0:T(8,128)S(1)} %copy.10.row_s, s32[8,1]{1,0:T(8,128)S(1)} %copy.11.edge_s, f32[2,128]{1,0:T(2,128)S(1)} %copy-done.3, s32[2,128]{1,0:T(2,128)S(1)} %copy-done.4, ...), custom_call_target="tpu_custom_call" | custom-call | flops 268435456 | bytes 2359296 | tf_op jit(solution)/shard_map/pallas_call | solution.py:441
  70.6 0.8 %copy.13 = f32[512,256]{1,0:T(8,128)} copy(f32[512,256]{1,0:T(8,128)S(1)} %shard_map.82) | data formatting | bytes 1048576
Async XLA Ops:
  2.2 1.6 %copy-start = (f32[2048,256]{1,0:T(8,128)S(1)}, f32[2048,256]{1,0:T(8,128)}, u32[]{:S(2)}) copy-start(f32[2048,256]{1,0:T(8,128)} %feat.1) | copy-start | bytes 6291460
  3.8 0.9 %copy-start.1 = (bf16[8,128,128]{2,1,0:T(8,128)(2,1)S(1)}, bf16[8,128,128]{2,1,0:T(8,128)(2,1)}, u32[]{:S(2)}) copy-start(bf16[8,128,128]{2,1,0:T(8,128)(2,1)} %inc.1) | copy-start | bytes 786436
  4.7 0.7 copy-start.2
  5.4 0.7 copy-start.3
  6.1 0.7 copy-start.4

commit v2 on v1

v2 whole, which is shorter than its diff:
```python
import functools
import math

import jax
import jax.numpy as jnp
from jax import lax
from jax.experimental import pallas as pl
from jax.experimental.pallas import tpu as pltpu
from jax.sharding import PartitionSpec as P

MESH = pl.DeviceIdType.MESH
LANES = 128
BF16 = jnp.bfloat16
F32 = jnp.float32


def repeat(start, stop, body):
    if stop - start <= 8:
        for step in range(start, stop):
            body(step)
    else:

        @pl.loop(start, stop)
        def _(step):
            body(step)


def kernel(
    nv,
    ne,
    chunks,
    feat,
    inc,
    live_s,
    row_s,
    edge_s,
    weight,
    degree,
    vdeg,
    out,
    mine,
    weight_v,
    degree_v,
    vdeg_v,
    tiles,
    meta_e,
    scale_e,
    meta_v,
    keys,
    owner_blocks,
    xs,
    rs,
    fwd_send,
    fwd_recv,
    bwd_send,
    bwd_recv,
    acc,
    prev,
    last,
    hyper_acc,
    hyper_feat,
    fin_send,
    fin_recv,
    meta_send_sem,
    meta_recv_sem,
    scale_send_sem,
    scale_recv_sem,
    tile_send_sem,
    tile_recv_sem,
    relay_sem,
    mv_send_sem,
    mv_recv_sem,
    fwd_send_sem,
    fwd_recv_sem,
    bwd_send_sem,
    bwd_recv_sem,
    fin_send_sem,
    fin_recv_sem,
    local_sem,
):
    v = lax.axis_index("vert")
    e = lax.axis_index("edge")
    block = inc.shape[1]
    blocks = xs.shape[1]
    part_cols = xs.shape[2]
    cols = chunks * part_cols
    hyper_blocks = weight.shape[0]
    share = blocks // ne
    none = nv * ne
    sibling = e + 1 - 2 * (e % 2)

    def edge_at(j):
        base = e + (j % 2) * (sibling - e)
        return (base + 2 * (j // 2)) % ne

    def pair_at(m):
        return pl.ds((e - e % 2 + 2 * m) % ne, 2)

    def to_edge(src, dst, send_sem, recv_sem, target):
        return pltpu.make_async_remote_copy(
            src_ref=src,
            dst_ref=dst,
            send_sem=send_sem,
            recv_sem=recv_sem,
            device_id=(v, target),
            device_id_type=MESH,
        )

    def to_vert(src, dst, send_sem, recv_sem, target):
        return pltpu.make_async_remote_copy(
            src_ref=src,
            dst_ref=dst,
            send_sem=send_sem,
            recv_sem=recv_sem,
            device_id=(target, e),
            device_id_type=MESH,
        )

    group = LANES // cols
    start = pl.multiple_of((e // group) * LANES, LANES)
    part = e % group
    fetches = [
        pltpu.make_async_copy(weight, weight_v, local_sem.at[2]),
        pltpu.make_async_copy(degree, degree_v, local_sem.at[3]),
        pltpu.make_async_copy(vdeg, vdeg_v, local_sem.at[4]),
        pltpu.make_async_copy(feat.at[:, pl.ds(start, LANES)], mine, local_sem.at[5]),
        pltpu.make_async_copy(inc, tiles.at[e], local_sem.at[6]),
    ]
    for copy in fetches:
        copy.start()

    barrier = pltpu.get_barrier_semaphore()

    def greet_vert(t):
        pl.semaphore_signal(barrier, inc=1, device_id=((v + t) % nv, e), device_id_type=MESH)

    repeat(1, nv, greet_vert)
    for j in range(1, ne):
        pl.semaphore_signal(barrier, inc=1, device_id=(v, edge_at(j)), device_id_type=MESH)

    lane = lax.broadcasted_iota(jnp.int32, (8, LANES), 1)
    sub = lax.broadcasted_iota(jnp.int32, (8, LANES), 0)
    packed = jnp.zeros((8, LANES), jnp.int32)
    for s in range(nv):
        key = jnp.where(live_s[0, s] > 0, row_s[0, s], -1)
        both = jnp.where(sub == 0, key, edge_s[0, s])
        packed = jnp.where(lane == s, both, packed)
    meta_e[e] = packed
    for copy in fetches[:2]:
        copy.wait()
    scale_e[e, :hyper_blocks] = weight_v[...] / jnp.maximum(degree_v[...], 1).astype(F32)

    pl.semaphore_wait(barrier, nv - 1 + ne - 1)

    meta_copies, tile_copies = [], []
    for j in range(1, ne):
        target = edge_at(j)
        meta_copies.append(
            to_edge(
                meta_e.at[e], meta_e.at[e], meta_send_sem.at[j], meta_recv_sem.at[e], target
            )
        )
        meta_copies.append(
            to_edge(
                scale_e.at[e], scale_e.at[e], scale_send_sem.at[j], scale_recv_sem.at[e], target
            )
        )
    for copy in meta_copies:
        copy.start()
    for j in [1] + list(range(2, ne, 2)):
        copy = to_edge(
            inc, tiles.at[e], tile_send_sem.at[j], tile_recv_sem.at[e], edge_at(j)
        )
        copy.start()
        tile_copies.append(copy)

    for copy in fetches[2:4]:
        copy.wait()
    rs[...] = 1.0 / jnp.sqrt(jnp.maximum(vdeg_v[...], 1).astype(F32))
    for b in range(blocks):
        turned = mine[pl.ds(b * block, block), :].T
        picked = turned[:cols]
        for g in range(1, group):
            picked = jnp.where(part == g, turned[g * cols : (g + 1) * cols], picked)
        picked = (picked * rs[b : b + 1, :]).astype(BF16)
        for c in range(chunks):
            xs[c, b] = picked[c * part_cols : (c + 1) * part_cols]
    fetches[4].wait()

    def slot_of(j, s):
        if j == 0:
            return live_s[0, s] > 0, row_s[0, s]
        key = keys[edge_at(j), 0, s]
        return key >= 0, jnp.maximum(key, 0)

    def partial(j, s, some):
        alive, row = slot_of(j, s)
        held = [xs[c, row] for c in some]
        left = held[0] if len(held) == 1 else jnp.concatenate(held, axis=0)
        value = jnp.dot(left, tiles[edge_at(j), s], preferred_element_type=F32)
        return jnp.where(alive, value, 0.0).astype(BF16)

    def fwd_copy(c, t):
        return to_vert(
            fwd_send.at[c, t],
            fwd_recv.at[c, v],
            fwd_send_sem.at[c, t],
            fwd_recv_sem.at[c, v],
            (v + t) % nv,
        )

    def fwd_arrival(c, source):
        return to_vert(
            fwd_send.at[c, 0],
            fwd_recv.at[c, source],
            fwd_send_sem.at[c, 0],
            fwd_recv_sem.at[c, source],
            v,
        )

    def bwd_copy(c, t):
        return to_vert(
            bwd_send.at[c, t],
            bwd_recv.at[c, v],
            bwd_send_sem.at[c, t],
            bwd_recv_sem.at[c, v],
            (v + t) % nv,
        )

    def bwd_arrival(c, source):
        return to_vert(
            bwd_send.at[c, 0],
            bwd_recv.at[c, source],
            bwd_send_sem.at[c, 0],
            bwd_recv_sem.at[c, source],
            v,
        )

    def mv_copy(t):
        return to_vert(
            meta_v.at[v], meta_v.at[v], mv_send_sem.at[t], mv_recv_sem.at[v], (v + t) % nv
        )

    def mv_arrival(source):
        return to_vert(
            meta_v.at[v], meta_v.at[source], mv_send_sem.at[0], mv_recv_sem.at[source], v
        )

    def tile_arrival(source):
        return to_edge(inc, tiles.at[source], tile_send_sem.at[0], tile_recv_sem.at[source], e)

    def first_part(j):
        here = edge_at(j)

        def step(t):
            value = partial(j, (v + t) % nv, range(chunks))
            for c in range(chunks):
                fwd_send[c, t, here] = value[c * part_cols : (c + 1) * part_cols]

        repeat(1, nv, step)
        value = partial(j, v, range(chunks))
        for c in range(chunks):
            fwd_recv[c, v, here] = value[c * part_cols : (c + 1) * part_cols]

    def first_pair(m):
        pair = pair_at(m)

        for c in range(chunks):

            def step(t):
                to_vert(
                    fwd_send.at[c, t, pair],
                    fwd_recv.at[c, v, pair],
                    fwd_send_sem.at[c, t],
                    fwd_recv_sem.at[c, v],
                    (v + t) % nv,
                ).start()

            repeat(1, nv, step)

    first_part(0)

    for j in range(1, ne):
        source = edge_at(j)
        to_edge(
            meta_e.at[e], meta_e.at[source], meta_send_sem.at[0], meta_recv_sem.at[source], e
        ).wait_recv()
        to_edge(
            scale_e.at[e], scale_e.at[source], scale_send_sem.at[0], scale_recv_sem.at[source], e
        ).wait_recv()
    to_scalars = pltpu.make_async_copy(meta_e, keys, local_sem.at[0])
    to_scalars.start()
    seen = jnp.zeros((8, LANES), jnp.int32)
    for other in range(ne):
        seen = jnp.where(sub == other, meta_e[other, 1:2, :], seen)
    meta_v[v] = seen
    repeat(1, nv, lambda t: mv_copy(t).start())
    to_scalars.wait()

    relays = []
    for j in range(1, ne):
        source = edge_at(j)
        tile_arrival(source).wait_recv()
        if j >= 2 and j % 2 == 0:
            copy = to_edge(
                tiles.at[source],
                tiles.at[source],
                relay_sem.at[j],
                tile_recv_sem.at[source],
                sibling,
            )
            copy.start()
            relays.append(copy)
        first_part(j)
        if j % 2:
            first_pair(j // 2)

    def link(i, latest):
        key = keys[edge_at(i % ne), 0, (v - i // ne + nv) % nv]
        before = none
        for b in range(blocks):
            before = jnp.where(key == b, latest[b], before)
        prev[i] = before
        return tuple(jnp.where(key == b, i, latest[b]) for b in range(blocks))

    latest = lax.fori_loop(0, none, link, (jnp.int32(none),) * blocks)
    for b in range(blocks):
        last[b] = latest[b]
    for c in range(chunks):
        acc[c, none] = jnp.zeros(acc.shape[2:], F32)

    repeat(1, nv, lambda t: mv_arrival((v - t + nv) % nv).wait_recv())
    to_scalars = pltpu.make_async_copy(meta_v, owner_blocks, local_sem.at[1])
    to_scalars.start()
    to_scalars.wait()

    def send_again(c):
        def send_all(t):
            for j in range(ne):
                fwd_send[c, t, edge_at(j)] = partial(j, (v + t) % nv, (c,))
            fwd_copy(c, t).start()

        repeat(1, nv, send_all)
        for j in range(ne):
            fwd_recv[c, v, edge_at(j)] = partial(j, v, (c,))

    def answer_all(c, applied):
        def add_from(source, first):
            for other in range(ne):
                held = owner_blocks[source, other, v]
                value = fwd_recv[c, source, other].astype(F32)
                for h in range(hyper_blocks):
                    term = jnp.where(held == h, value, 0.0)
                    hyper_acc[h, other] = term if first else hyper_acc[h, other] + term

        add_from(v, True)

        def arrive(t):
            source = (v - t + nv) % nv
            fwd_arrival(c, source).wait_recv()
            add_from(source, False)

        repeat(1, nv, arrive)
        for other in range(ne):
            for h in range(hyper_blocks):
                hyper_feat[h, other] = (
                    hyper_acc[h, other] * scale_e[other, h : h + 1, :]
                ).astype(BF16)

        def answer(t):
            if applied:
                bwd_copy(c, t).wait_send()
            for other in range(ne):
                held = owner_blocks[(v + t) % nv, other, v]
                bwd_send[c, t, other] = hyper_feat[held, other]
            bwd_copy(c, t).start()

        repeat(1, nv, answer)
        for other in range(ne):
            bwd_recv[c, v, other] = hyper_feat[owner_blocks[v, other, v], other]
        repeat(1, nv, lambda t: fwd_copy(c, t).wait_send())

    def gather_rows(c):
        def spread(t):
            slot = (v - t + nv) % nv
            for j in range(ne):
                i = t * ne + j
                value = lax.dot_general(
                    bwd_recv[c, slot, edge_at(j)],
                    tiles[edge_at(j), slot],
                    (((1,), (1,)), ((), ())),
                    preferred_element_type=F32,
                )
                acc[c, i] = value + acc[c, prev[i]]

        spread(0)

        def come_back(t):
            bwd_arrival(c, (v - t + nv) % nv).wait_recv()
            spread(t)

        repeat(1, nv, come_back)

    def fin_copy(c, j):
        return to_edge(
            fin_send.at[c, j],
            fin_recv.at[c, e],
            fin_send_sem.at[c, j],
            fin_recv_sem.at[c, e],
            edge_at(j),
        )

    def finish(c):
        for j in range(ne - 1, -1, -1):
            for k in range(share):
                b = edge_at(j) * share + k
                value = (rs[pl.ds(b, 1), :] * acc[c, last[b]]).astype(BF16)
                if j:
                    fin_send[c, j, k] = value
                else:
                    fin_recv[c, e, k] = value
            if j:
                fin_copy(c, j).start()

    for applied in range(2):
        for c in range(chunks):
            answer_all(c, applied)
        for c in range(chunks):
            gather_rows(c)
            if applied:
                finish(c)
            else:
                for b in range(blocks):
                    scale = rs[b : b + 1, :]
                    xs[c, b] = (scale * (scale * acc[c, last[b]])).astype(BF16)
                send_again(c)

    for c in range(chunks):
        for j in range(1, ne):
            source = edge_at(j)
            to_edge(
                fin_send.at[c, 0],
                fin_recv.at[c, source],
                fin_send_sem.at[c, 0],
                fin_recv_sem.at[c, source],
                e,
            ).wait_recv()
    for k in range(share):
        for g in range(ne // group):
            stacked = jnp.concatenate(
                [
                    fin_recv[c, g * group + i, k].astype(F32)
                    for i in range(group)
                    for c in range(chunks)
                ],
                axis=0,
            )
            out[pl.ds(k * block, block), pl.ds(g * LANES, LANES)] = stacked.T

    for copy in meta_copies + tile_copies + relays:
        copy.wait_send()
    repeat(1, nv, lambda t: mv_copy(t).wait_send())
    for c in range(chunks):
        repeat(1, nv, lambda t: bwd_copy(c, t).wait_send())
        for j in range(1, ne):
            fin_copy(c, j).wait_send()


def shards(
    features, incidence, send_count, row_block, edge_block, edge_weight, edge_degree, vertex_degree
):
    nv = lax.axis_size("vert")
    ne = lax.axis_size("edge")
    papers, width = features.shape
    slots, block, _ = incidence.shape
    blocks = papers // block
    hyper_blocks = edge_weight.shape[0]
    cols = width // ne
    share = blocks // ne
    chunks = max(1, cols // 32)
    cut = cols // chunks
    scratch = [
        ((papers, LANES), F32),
        ((hyper_blocks, block), F32),
        ((hyper_blocks, block), jnp.int32),
        ((blocks, block), jnp.int32),
        ((ne, slots, block, block), BF16),
        ((ne, 8, LANES), jnp.int32),
        ((ne, 8, LANES), F32),
        ((nv, 8, LANES), jnp.int32),
        None,
        None,
        ((chunks, blocks, cut, block), BF16),
        ((blocks, block), F32),
        ((chunks, nv, ne, cut, block), BF16),
        ((chunks, nv, ne, cut, block), BF16),
        ((chunks, nv, ne, cut, block), BF16),
        ((chunks, nv, ne, cut, block), BF16),
        ((chunks, nv * ne + 1, cut, block), F32),
        None,
        None,
        ((hyper_blocks, ne, cut, block), F32),
        ((hyper_blocks, ne, cut, block), BF16),
        ((chunks, ne, share, cut, block), BF16),
        ((chunks, ne, share, cut, block), BF16),
    ]
    scalars = iter(
        [(ne, 8, LANES), (nv, 8, LANES), (nv * ne,), (blocks,)]
    )
    held = sum(
        math.prod(item[0]) * jnp.dtype(item[1]).itemsize for item in scratch if item is not None
    )
    held += papers // ne * width * 4
    shapes = [
        pltpu.SMEM(next(scalars), jnp.int32) if item is None else pltpu.VMEM(*item)
        for item in scratch
    ]
    dma = pltpu.SemaphoreType.DMA
    sems = [dma((ne,))] * 7 + [dma((nv,))] * 2 + [dma((chunks, nv))] * 4
    sems += [dma((chunks, ne))] * 2 + [dma((7,))]
    hbm = pl.BlockSpec(memory_space=pltpu.HBM)
    vmem = pl.BlockSpec(memory_space=pltpu.VMEM)
    smem = pl.BlockSpec(memory_space=pltpu.SMEM)
    return pl.pallas_call(
        functools.partial(kernel, nv, ne, chunks),
        out_shape=jax.ShapeDtypeStruct((papers // ne, width), F32),
        in_specs=[hbm, hbm, smem, smem, smem, hbm, hbm, hbm],
        out_specs=vmem,
        scratch_shapes=shapes + sems,
        compiler_params=pltpu.CompilerParams(
            collective_id=0,
            has_side_effects=True,
            vmem_limit_bytes=max(held + 6 * 2**20, 60 * 2**20),
        ),
        cost_estimate=pl.CostEstimate(
            flops=8 * slots * ne * block * block * cols,
            bytes_accessed=features.size * 4 + incidence.size * 2,
            transcendentals=0,
        ),
    )(
        features,
        incidence,
        send_count.reshape(1, slots),
        row_block.reshape(1, slots),
        edge_block.reshape(1, slots),
        edge_weight,
        edge_degree,
        vertex_degree.reshape(blocks, block),
    )


def solution(mesh):
    placed = (
        P("vert", None),
        P("vert", None, "edge"),
        P("vert", "edge"),
        P("vert", "edge"),
        P("vert", "edge"),
        P("vert", "edge"),
        P("vert", "edge"),
        P("vert"),
    )
    return jax.shard_map(
        shards, mesh=mesh, in_specs=placed, out_specs=P(("vert", "edge"), None), check_vma=False
    )
```

time: 71.6 us -> 65.8 us (0.919)
  local copies, waits for them, and re-layouts: 7.58 us -> 1.87 us
    unnamed x14 -> x1, local copies, waits for them, and re-layouts: 7.58 us -> 1.87 us
where the time goes in v2:
time: 65.8 us; the launch traced here: 65.6 us
  Pallas kernels  63.7 us (97%)
  local copies, waits for them, and re-layouts  1.87 us (3%)
    pallas_call x1, Pallas kernels, shards(): pl.pallas_call(functools.partial(kernel, nv, ne, chunks), out_shape=jax.S...  63.7 us
    unnamed x1, local copies, waits for them, and re-layouts  1.87 us

profile of v2, /device:TPU:0, one launch (start us, length us, event | category | flops | bytes accessed | tf_op | source)
XLA Modules:
  0.0 65.6 jit_solution(3945786016744271363)
XLA Ops:
  0.0 63.7 %shard_map.82 = f32[512,256]{1,0:T(8,128)} custom-call(f32[2048,256]{1,0:T(8,128)} %feat.1, bf16[8,128,128]{2,1,0:T(8,128)(2,1)} %inc.1, s32[1,8]{1,0:T(1,128)} %bitcast.5, s32[1,8]{1,0:T(1,128)} %bitcast.6, s32[1,8]{1,0:T(1,128)} %bitcast.7, f32[2,128]{1,0:T(2,128)} %weight.1, s32[2,128]{1,0:T(2,128)} %degree.1, s32[16,128]{1,0:T(8,128)} %bitcast.4), custom_call_target="tpu_custom_call" | custom-call | flops 268435456 | bytes 2359296 | tf_op jit(solution)/shard_map/pallas_call | solution.py:524
  63.7 1.9 %copy.10 = f32[512,256]{1,0:T(8,128)} copy(f32[512,256]{1,0:T(8,128)} %shard_map.82) | data formatting | bytes 1048576

commit v3 on v2

--- a/solution.py
+++ b/solution.py
@@ -45,6 +45,7 @@
     tiles,
     meta_e,
     scale_e,
+    scale_m,
     meta_v,
     keys,
     owner_blocks,
@@ -59,6 +60,8 @@
     last,
     hyper_acc,
     hyper_feat,
+    mir_send,
+    mir_recv,
     fin_send,
     fin_recv,
     meta_send_sem,
@@ -76,6 +79,8 @@
     bwd_recv_sem,
     fin_send_sem,
     fin_recv_sem,
+    mir_send_sem,
+    mir_recv_sem,
     local_sem,
 ):
     v = lax.axis_index("vert")
@@ -87,14 +92,24 @@
     hyper_blocks = weight.shape[0]
     share = blocks // ne
     none = nv * ne
+    half = nv // 2
+    here = v % half
+    base = v - here
+    mirror = (v + half) % nv
     sibling = e + 1 - 2 * (e % 2)
 
     def edge_at(j):
-        base = e + (j % 2) * (sibling - e)
-        return (base + 2 * (j // 2)) % ne
+        first = e + (j % 2) * (sibling - e)
+        return (first + 2 * (j // 2)) % ne
 
     def pair_at(m):
         return pl.ds((e - e % 2 + 2 * m) % ne, 2)
+
+    def ahead(t):
+        return base + (here + t) % half
+
+    def behind(t):
+        return (here - t + half) % half
 
     def to_edge(src, dst, send_sem, recv_sem, target):
         return pltpu.make_async_remote_copy(
@@ -132,9 +147,10 @@
     barrier = pltpu.get_barrier_semaphore()
 
     def greet_vert(t):
-        pl.semaphore_signal(barrier, inc=1, device_id=((v + t) % nv, e), device_id_type=MESH)
-
-    repeat(1, nv, greet_vert)
+        pl.semaphore_signal(barrier, inc=1, device_id=(ahead(t), e), device_id_type=MESH)
+
+    repeat(1, half, greet_vert)
+    pl.semaphore_signal(barrier, inc=1, device_id=(mirror, e), device_id_type=MESH)
     for j in range(1, ne):
         pl.semaphore_signal(barrier, inc=1, device_id=(v, edge_at(j)), device_id_type=MESH)
 
@@ -150,7 +166,7 @@
         copy.wait()
     scale_e[e, :hyper_blocks] = weight_v[...] / jnp.maximum(degree_v[...], 1).astype(F32)
 
-    pl.semaphore_wait(barrier, nv - 1 + ne - 1)
+    pl.semaphore_wait(barrier, half + ne - 1)
 
     meta_copies, tile_copies = [], []
     for j in range(1, ne):
@@ -203,10 +219,10 @@
     def fwd_copy(c, t):
         return to_vert(
             fwd_send.at[c, t],
-            fwd_recv.at[c, v],
+            fwd_recv.at[c, here],
             fwd_send_sem.at[c, t],
-            fwd_recv_sem.at[c, v],
-            (v + t) % nv,
+            fwd_recv_sem.at[c, here],
+            ahead(t),
         )
 
     def fwd_arrival(c, source):
@@ -221,10 +237,10 @@
     def bwd_copy(c, t):
         return to_vert(
             bwd_send.at[c, t],
-            bwd_recv.at[c, v],
+            bwd_recv.at[c, here],
             bwd_send_sem.at[c, t],
-            bwd_recv_sem.at[c, v],
-            (v + t) % nv,
+            bwd_recv_sem.at[c, here],
+            ahead(t),
         )
 
     def bwd_arrival(c, source):
@@ -238,29 +254,40 @@
 
     def mv_copy(t):
         return to_vert(
-            meta_v.at[v], meta_v.at[v], mv_send_sem.at[t], mv_recv_sem.at[v], (v + t) % nv
+            meta_v.at[here], meta_v.at[here], mv_send_sem.at[t], mv_recv_sem.at[here], ahead(t)
         )
 
     def mv_arrival(source):
         return to_vert(
-            meta_v.at[v], meta_v.at[source], mv_send_sem.at[0], mv_recv_sem.at[source], v
+            meta_v.at[here], meta_v.at[source], mv_send_sem.at[0], mv_recv_sem.at[source], v
         )
 
     def tile_arrival(source):
         return to_edge(inc, tiles.at[source], tile_send_sem.at[0], tile_recv_sem.at[source], e)
 
+    def mir_copy(p):
+        return to_vert(
+            mir_send.at[p], mir_recv.at[p], mir_send_sem.at[p], mir_recv_sem.at[p], mirror
+        )
+
+    scale_copy = to_vert(
+        scale_e, scale_m, mir_send_sem.at[2 * chunks], mir_recv_sem.at[2 * chunks], mirror
+    )
+
     def first_part(j):
-        here = edge_at(j)
+        other = edge_at(j)
 
         def step(t):
-            value = partial(j, (v + t) % nv, range(chunks))
+            for q in range(2):
+                value = partial(j, q * half + (here + t) % half, range(chunks))
+                for c in range(chunks):
+                    fwd_send[c, t, other, q] = value[c * part_cols : (c + 1) * part_cols]
+
+        repeat(1, half, step)
+        for q in range(2):
+            value = partial(j, q * half + here, range(chunks))
             for c in range(chunks):
-                fwd_send[c, t, here] = value[c * part_cols : (c + 1) * part_cols]
-
-        repeat(1, nv, step)
-        value = partial(j, v, range(chunks))
-        for c in range(chunks):
-            fwd_recv[c, v, here] = value[c * part_cols : (c + 1) * part_cols]
+                fwd_recv[c, here, other, q] = value[c * part_cols : (c + 1) * part_cols]
 
     def first_pair(m):
         pair = pair_at(m)
@@ -270,13 +297,13 @@
             def step(t):
                 to_vert(
                     fwd_send.at[c, t, pair],
-                    fwd_recv.at[c, v, pair],
+                    fwd_recv.at[c, here, pair],
                     fwd_send_sem.at[c, t],
-                    fwd_recv_sem.at[c, v],
-                    (v + t) % nv,
+                    fwd_recv_sem.at[c, here],
+                    ahead(t),
                 ).start()
 
-            repeat(1, nv, step)
+            repeat(1, half, step)
 
     first_part(0)
 
@@ -293,8 +320,9 @@
     seen = jnp.zeros((8, LANES), jnp.int32)
     for other in range(ne):
         seen = jnp.where(sub == other, meta_e[other, 1:2, :], seen)
-    meta_v[v] = seen
-    repeat(1, nv, lambda t: mv_copy(t).start())
+    meta_v[here] = seen
+    repeat(1, half, lambda t: mv_copy(t).start())
+    scale_copy.start()
     to_scalars.wait()
 
     relays = []
@@ -316,7 +344,8 @@
             first_pair(j // 2)
 
     def link(i, latest):
-        key = keys[edge_at(i % ne), 0, (v - i // ne + nv) % nv]
+        slot = ((i // ne) % 2) * half + behind(i // (2 * ne))
+        key = keys[edge_at(i % ne), 0, slot]
         before = none
         for b in range(blocks):
             before = jnp.where(key == b, latest[b], before)
@@ -329,7 +358,7 @@
     for c in range(chunks):
         acc[c, none] = jnp.zeros(acc.shape[2:], F32)
 
-    repeat(1, nv, lambda t: mv_arrival((v - t + nv) % nv).wait_recv())
+    repeat(1, half, lambda t: mv_arrival(behind(t)).wait_recv())
     to_scalars = pltpu.make_async_copy(meta_v, owner_blocks, local_sem.at[1])
     to_scalars.start()
     to_scalars.wait()
@@ -337,69 +366,88 @@
     def send_again(c):
         def send_all(t):
             for j in range(ne):
-                fwd_send[c, t, edge_at(j)] = partial(j, (v + t) % nv, (c,))
+                for q in range(2):
+                    slot = q * half + (here + t) % half
+                    fwd_send[c, t, edge_at(j), q] = partial(j, slot, (c,))
             fwd_copy(c, t).start()
 
-        repeat(1, nv, send_all)
+        repeat(1, half, send_all)
         for j in range(ne):
-            fwd_recv[c, v, edge_at(j)] = partial(j, v, (c,))
-
-    def answer_all(c, applied):
+            for q in range(2):
+                fwd_recv[c, here, edge_at(j), q] = partial(j, q * half + here, (c,))
+
+    def sum_half(c, applied):
         def add_from(source, first):
             for other in range(ne):
-                held = owner_blocks[source, other, v]
-                value = fwd_recv[c, source, other].astype(F32)
+                for q in range(2):
+                    held = owner_blocks[source, other, q * half + here]
+                    value = fwd_recv[c, source, other, q].astype(F32)
+                    for h in range(hyper_blocks):
+                        term = jnp.where(held == h, value, 0.0)
+                        if not first:
+                            term = hyper_acc[c, q, h, other] + term
+                        hyper_acc[c, q, h, other] = term
+
+        add_from(here, True)
+
+        def arrive(t):
+            fwd_arrival(c, behind(t)).wait_recv()
+            add_from(behind(t), False)
+
+        repeat(1, half, arrive)
+        mir_send[applied * chunks + c] = hyper_acc[c].astype(BF16)
+        mir_copy(applied * chunks + c).start()
+        repeat(1, half, lambda t: fwd_copy(c, t).wait_send())
+
+    def answer_all(c, applied):
+        mir_copy(applied * chunks + c).wait_recv()
+        if c == 0 and not applied:
+            scale_copy.wait_recv()
+        for q in range(2):
+            own = q == v // half
+            for other in range(ne):
+                scale = jnp.where(own, scale_e[other], scale_m[other])
                 for h in range(hyper_blocks):
-                    term = jnp.where(held == h, value, 0.0)
-                    hyper_acc[h, other] = term if first else hyper_acc[h, other] + term
-
-        add_from(v, True)
-
-        def arrive(t):
-            source = (v - t + nv) % nv
-            fwd_arrival(c, source).wait_recv()
-            add_from(source, False)
-
-        repeat(1, nv, arrive)
-        for other in range(ne):
-            for h in range(hyper_blocks):
-                hyper_feat[h, other] = (
-                    hyper_acc[h, other] * scale_e[other, h : h + 1, :]
-                ).astype(BF16)
+                    total = hyper_acc[c, q, h, other] + mir_recv[
+                        applied * chunks + c, q, h, other
+                    ].astype(F32)
+                    hyper_feat[q, h, other] = (total * scale[h : h + 1, :]).astype(BF16)
 
         def answer(t):
             if applied:
                 bwd_copy(c, t).wait_send()
             for other in range(ne):
-                held = owner_blocks[(v + t) % nv, other, v]
-                bwd_send[c, t, other] = hyper_feat[held, other]
+                for q in range(2):
+                    held = owner_blocks[(here + t) % half, other, q * half + here]
+                    bwd_send[c, t, other, q] = hyper_feat[q, held, other]
             bwd_copy(c, t).start()
 
-        repeat(1, nv, answer)
+        repeat(1, half, answer)
         for other in range(ne):
-            bwd_recv[c, v, other] = hyper_feat[owner_blocks[v, other, v], other]
-        repeat(1, nv, lambda t: fwd_copy(c, t).wait_send())
+            for q in range(2):
+                held = owner_blocks[here, other, q * half + here]
+                bwd_recv[c, here, other, q] = hyper_feat[q, held, other]
 
     def gather_rows(c):
         def spread(t):
-            slot = (v - t + nv) % nv
-            for j in range(ne):
-                i = t * ne + j
-                value = lax.dot_general(
-                    bwd_recv[c, slot, edge_at(j)],
-                    tiles[edge_at(j), slot],
-                    (((1,), (1,)), ((), ())),
-                    preferred_element_type=F32,
-                )
-                acc[c, i] = value + acc[c, prev[i]]
+            for q in range(2):
+                for j in range(ne):
+                    i = t * 2 * ne + q * ne + j
+                    value = lax.dot_general(
+                        bwd_recv[c, behind(t), edge_at(j), q],
+                        tiles[edge_at(j), q * half + behind(t)],
+                        (((1,), (1,)), ((), ())),
+                        preferred_element_type=F32,
+                    )
+                    acc[c, i] = value + acc[c, prev[i]]
 
         spread(0)
 
         def come_back(t):
-            bwd_arrival(c, (v - t + nv) % nv).wait_recv()
+            bwd_arrival(c, behind(t)).wait_recv()
             spread(t)
 
-        repeat(1, nv, come_back)
+        repeat(1, half, come_back)
 
     def fin_copy(c, j):
         return to_edge(
@@ -423,6 +471,8 @@
                 fin_copy(c, j).start()
 
     for applied in range(2):
+        for c in range(chunks):
+            sum_half(c, applied)
         for c in range(chunks):
             answer_all(c, applied)
         for c in range(chunks):
@@ -455,13 +505,16 @@
                 ],
                 axis=0,
             )
-            out[pl.ds(k * block, block), pl.ds(g * LANES, LANES)] = stacked.T
+            out[pl.ds(k * block, block), pl.ds(g * LANES, LANES)] = stacked.T.astype(BF16)
 
     for copy in meta_copies + tile_copies + relays:
         copy.wait_send()
-    repeat(1, nv, lambda t: mv_copy(t).wait_send())
+    repeat(1, half, lambda t: mv_copy(t).wait_send())
+    scale_copy.wait_send()
     for c in range(chunks):
-        repeat(1, nv, lambda t: bwd_copy(c, t).wait_send())
+        for applied in range(2):
+            mir_copy(applied * chunks + c).wait_send()
+        repeat(1, half, lambda t: bwd_copy(c, t).wait_send())
         for j in range(1, ne):
             fin_copy(c, j).wait_send()
 
@@ -477,6 +530,7 @@
     hyper_blocks = edge_weight.shape[0]
     cols = width // ne
     share = blocks // ne
+    half = nv // 2
     chunks = max(1, cols // 32)
     cut = cols // chunks
     scratch = [
@@ -487,43 +541,46 @@
         ((ne, slots, block, block), BF16),
         ((ne, 8, LANES), jnp.int32),
         ((ne, 8, LANES), F32),
-        ((nv, 8, LANES), jnp.int32),
+        ((ne, 8, LANES), F32),
+        ((half, 8, LANES), jnp.int32),
         None,
         None,
         ((chunks, blocks, cut, block), BF16),
         ((blocks, block), F32),
-        ((chunks, nv, ne, cut, block), BF16),
-        ((chunks, nv, ne, cut, block), BF16),
-        ((chunks, nv, ne, cut, block), BF16),
-        ((chunks, nv, ne, cut, block), BF16),
+        ((chunks, half, ne, 2, cut, block), BF16),
+        ((chunks, half, ne, 2, cut, block), BF16),
+        ((chunks, half, ne, 2, cut, block), BF16),
+        ((chunks, half, ne, 2, cut, block), BF16),
         ((chunks, nv * ne + 1, cut, block), F32),
         None,
         None,
-        ((hyper_blocks, ne, cut, block), F32),
-        ((hyper_blocks, ne, cut, block), BF16),
+        ((chunks, 2, hyper_blocks, ne, cut, block), F32),
+        ((2, hyper_blocks, ne, cut, block), BF16),
+        ((2 * chunks, 2, hyper_blocks, ne, cut, block), BF16),
+        ((2 * chunks, 2, hyper_blocks, ne, cut, block), BF16),
         ((chunks, ne, share, cut, block), BF16),
         ((chunks, ne, share, cut, block), BF16),
     ]
     scalars = iter(
-        [(ne, 8, LANES), (nv, 8, LANES), (nv * ne,), (blocks,)]
+        [(ne, 8, LANES), (half, 8, LANES), (nv * ne,), (blocks,)]
     )
     held = sum(
         math.prod(item[0]) * jnp.dtype(item[1]).itemsize for item in scratch if item is not None
     )
-    held += papers // ne * width * 4
+    held += papers // ne * width * 2
     shapes = [
         pltpu.SMEM(next(scalars), jnp.int32) if item is None else pltpu.VMEM(*item)
         for item in scratch
     ]
     dma = pltpu.SemaphoreType.DMA
-    sems = [dma((ne,))] * 7 + [dma((nv,))] * 2 + [dma((chunks, nv))] * 4
-    sems += [dma((chunks, ne))] * 2 + [dma((7,))]
+    sems = [dma((ne,))] * 7 + [dma((half,))] * 2 + [dma((chunks, half))] * 4
+    sems += [dma((chunks, ne))] * 2 + [dma((2 * chunks + 1,))] * 2 + [dma((7,))]
     hbm = pl.BlockSpec(memory_space=pltpu.HBM)
     vmem = pl.BlockSpec(memory_space=pltpu.VMEM)
     smem = pl.BlockSpec(memory_space=pltpu.SMEM)
     return pl.pallas_call(
         functools.partial(kernel, nv, ne, chunks),
-        out_shape=jax.ShapeDtypeStruct((papers // ne, width), F32),
+        out_shape=jax.ShapeDtypeStruct((papers // ne, width), BF16),
         in_specs=[hbm, hbm, smem, smem, smem, hbm, hbm, hbm],
         out_specs=vmem,
         scratch_shapes=shapes + sems,
@@ -546,7 +603,7 @@
         edge_weight,
         edge_degree,
         vertex_degree.reshape(blocks, block),
-    )
+    ).astype(F32)
 
 
 def solution(mesh):

time: 65.8 us -> 64.9 us (0.986)
  local copies, waits for them, and re-layouts: 1.87 us -> 0 us
  other arithmetic: 0 us -> 1.78 us
  Pallas kernels: 63.7 us -> 63 us
    unnamed x1 -> x0, local copies, waits for them, and re-layouts: 1.87 us -> none
    convert_element_type x0 -> x1, other arithmetic: none -> 1.78 us  [shards(): return pl.pallas_call(functools.partial(kernel, nv, ne, chunks), out_shap...]
    pallas_call x1, Pallas kernels: 63.7 us -> 63 us  [shards(): pl.pallas_call(functools.partial(kernel, nv, ne, chunks), out_shape=jax.S...]
where the time goes in v3:
time: 64.9 us; the launch traced here: 64.8 us
  Pallas kernels  63 us (97%)
  other arithmetic  1.78 us (3%)
    pallas_call x1, Pallas kernels, shards(): pl.pallas_call(functools.partial(kernel, nv, ne, chunks), out_shape=jax.S...  63 us
    convert_element_type x1, other arithmetic, shards(): return pl.pallas_call(functools.partial(kernel, nv, ne, chunks), out_shap...  1.78 us

profile of v3, /device:TPU:0, one launch (start us, length us, event | category | flops | bytes accessed | tf_op | source)
XLA Modules:
  0.0 64.8 jit_solution(16556450699988313510)
XLA Ops:
  0.0 63.0 %shard_map.82 = bf16[512,256]{1,0:T(8,128)(2,1)} custom-call(f32[2048,256]{1,0:T(8,128)} %feat.1, bf16[8,128,128]{2,1,0:T(8,128)(2,1)} %inc.1, s32[1,8]{1,0:T(1,128)} %bitcast.5, s32[1,8]{1,0:T(1,128)} %bitcast.6, s32[1,8]{1,0:T(1,128)} %bitcast.7, f32[2,128]{1,0:T(2,128)} %weight.1, s32[2,128]{1,0:T(2,128)} %degree.1, s32[16,128]{1,0:T(8,128)} %bitcast.4), custom_call_target="tpu_custom_call" | custom-call | flops 268435456 | bytes 2359296 | tf_op jit(solution)/shard_map/pallas_call | solution.py:581
  63.0 1.8 %convert_element_type.3 = f32[512,256]{1,0:T(8,128)} convert(bf16[512,256]{1,0:T(8,128)(2,1)} %shard_map.82) | non-fusion elementwise | flops 131072 | bytes 786432 | tf_op jit(solution)/shard_map/convert_element_type | solution.py:606

commit v4 on v3

--- a/solution.py
+++ b/solution.py
@@ -15,14 +15,9 @@
 
 
 def repeat(start, stop, body):
-    if stop - start <= 8:
-        for step in range(start, stop):
-            body(step)
-    else:
-
-        @pl.loop(start, stop)
-        def _(step):
-            body(step)
+    @pl.loop(start, stop)
+    def _(step):
+        body(step)
 
 
 def kernel(
@@ -184,23 +179,35 @@
     for copy in meta_copies:
         copy.start()
     for j in [1] + list(range(2, ne, 2)):
-        copy = to_edge(
-            inc, tiles.at[e], tile_send_sem.at[j], tile_recv_sem.at[e], edge_at(j)
-        )
-        copy.start()
-        tile_copies.append(copy)
+        for q in range(2):
+            some = pl.ds(q * half, half)
+            copy = to_edge(
+                inc.at[some],
+                tiles.at[e, some],
+                tile_send_sem.at[q, j],
+                tile_recv_sem.at[q, e],
+                edge_at(j),
+            )
+            copy.start()
+            tile_copies.append(copy)
 
     for copy in fetches[2:4]:
         copy.wait()
     rs[...] = 1.0 / jnp.sqrt(jnp.maximum(vdeg_v[...], 1).astype(F32))
-    for b in range(blocks):
-        turned = mine[pl.ds(b * block, block), :].T
-        picked = turned[:cols]
-        for g in range(1, group):
-            picked = jnp.where(part == g, turned[g * cols : (g + 1) * cols], picked)
-        picked = (picked * rs[b : b + 1, :]).astype(BF16)
-        for c in range(chunks):
-            xs[c, b] = picked[c * part_cols : (c + 1) * part_cols]
+    unit = math.gcd(blocks, 4)
+
+    def prepare(u):
+        for i in range(unit):
+            b = u * unit + i
+            turned = mine[pl.ds(pl.multiple_of(b * block, block), block), :].T
+            picked = turned[:cols]
+            for g in range(1, group):
+                picked = jnp.where(part == g, turned[g * cols : (g + 1) * cols], picked)
+            picked = (picked * rs[pl.ds(b, 1), :]).astype(BF16)
+            for c in range(chunks):
+                xs[c, b] = picked[c * part_cols : (c + 1) * part_cols]
+
+    repeat(0, blocks // unit, prepare)
     fetches[4].wait()
 
     def slot_of(j, s):
@@ -262,8 +269,15 @@
             meta_v.at[here], meta_v.at[source], mv_send_sem.at[0], mv_recv_sem.at[source], v
         )
 
-    def tile_arrival(source):
-        return to_edge(inc, tiles.at[source], tile_send_sem.at[0], tile_recv_sem.at[source], e)
+    def tile_arrival(q, source):
+        some = pl.ds(q * half, half)
+        return to_edge(
+            inc.at[some],
+            tiles.at[source, some],
+            tile_send_sem.at[q, 0],
+            tile_recv_sem.at[q, source],
+            e,
+        )
 
     def mir_copy(p):
         return to_vert(
@@ -274,20 +288,18 @@
         scale_e, scale_m, mir_send_sem.at[2 * chunks], mir_recv_sem.at[2 * chunks], mirror
     )
 
-    def first_part(j):
+    def first_part(j, q):
         other = edge_at(j)
 
         def step(t):
-            for q in range(2):
-                value = partial(j, q * half + (here + t) % half, range(chunks))
-                for c in range(chunks):
-                    fwd_send[c, t, other, q] = value[c * part_cols : (c + 1) * part_cols]
+            value = partial(j, q * half + (here + t) % half, range(chunks))
+            for c in range(chunks):
+                fwd_send[c, t, other, q] = value[c * part_cols : (c + 1) * part_cols]
 
         repeat(1, half, step)
-        for q in range(2):
-            value = partial(j, q * half + here, range(chunks))
-            for c in range(chunks):
-                fwd_recv[c, here, other, q] = value[c * part_cols : (c + 1) * part_cols]
+        value = partial(j, q * half + here, range(chunks))
+        for c in range(chunks):
+            fwd_recv[c, here, other, q] = value[c * part_cols : (c + 1) * part_cols]
 
     def first_pair(m):
         pair = pair_at(m)
@@ -305,7 +317,8 @@
 
             repeat(1, half, step)
 
-    first_part(0)
+    for q in range(2):
+        first_part(0, q)
 
     for j in range(1, ne):
         source = edge_at(j)
@@ -326,22 +339,33 @@
     to_scalars.wait()
 
     relays = []
-    for j in range(1, ne):
+    def relay(j, q):
         source = edge_at(j)
-        tile_arrival(source).wait_recv()
+        some = pl.ds(q * half, half)
+        tile_arrival(q, source).wait_recv()
         if j >= 2 and j % 2 == 0:
             copy = to_edge(
-                tiles.at[source],
-                tiles.at[source],
-                relay_sem.at[j],
-                tile_recv_sem.at[source],
+                tiles.at[source, some],
+                tiles.at[source, some],
+                relay_sem.at[q, j],
+                tile_recv_sem.at[q, source],
                 sibling,
             )
             copy.start()
             relays.append(copy)
-        first_part(j)
-        if j % 2:
-            first_pair(j // 2)
+
+    for q in range(2):
+        relay(1, q)
+        first_part(1, q)
+    first_pair(0)
+    for m in range(1, ne // 2):
+        for q in range(2):
+            relay(2 * m, q)
+            first_part(2 * m, q)
+        for q in range(2):
+            relay(2 * m + 1, q)
+            first_part(2 * m + 1, q)
+        first_pair(m)
 
     def link(i, latest):
         slot = ((i // ne) % 2) * half + behind(i // (2 * ne))
@@ -401,8 +425,6 @@
 
     def answer_all(c, applied):
         mir_copy(applied * chunks + c).wait_recv()
-        if c == 0 and not applied:
-            scale_copy.wait_recv()
         for q in range(2):
             own = q == v // half
             for other in range(ne):
@@ -414,8 +436,10 @@
                     hyper_feat[q, h, other] = (total * scale[h : h + 1, :]).astype(BF16)
 
         def answer(t):
-            if applied:
+            @pl.when(applied > 0)
+            def _():
                 bwd_copy(c, t).wait_send()
+
             for other in range(ne):
                 for q in range(2):
                     held = owner_blocks[(here + t) % half, other, q * half + here]
@@ -470,20 +494,36 @@
             if j:
                 fin_copy(c, j).start()
 
-    for applied in range(2):
-        for c in range(chunks):
-            sum_half(c, applied)
-        for c in range(chunks):
-            answer_all(c, applied)
-        for c in range(chunks):
+    def scale_again(c):
+        def rescale(u):
+            for i in range(unit):
+                b = u * unit + i
+                scale = rs[pl.ds(b, 1), :]
+                xs[c, b] = (scale * (scale * acc[c, last[b]])).astype(BF16)
+
+        repeat(0, blocks // unit, rescale)
+
+    scale_copy.wait_recv()
+
+    def one_pass(applied):
+        repeat(0, chunks, lambda c: sum_half(c, applied))
+        repeat(0, chunks, lambda c: answer_all(c, applied))
+
+        def rows(c):
             gather_rows(c)
-            if applied:
+
+            @pl.when(applied == 0)
+            def _():
+                scale_again(c)
+                send_again(c)
+
+            @pl.when(applied > 0)
+            def _():
                 finish(c)
-            else:
-                for b in range(blocks):
-                    scale = rs[b : b + 1, :]
-                    xs[c, b] = (scale * (scale * acc[c, last[b]])).astype(BF16)
-                send_again(c)
+
+        repeat(0, chunks, rows)
+
+    repeat(0, 2, one_pass)
 
     for c in range(chunks):
         for j in range(1, ne):
@@ -573,7 +613,7 @@
         for item in scratch
     ]
     dma = pltpu.SemaphoreType.DMA
-    sems = [dma((ne,))] * 7 + [dma((half,))] * 2 + [dma((chunks, half))] * 4
+    sems = [dma((ne,))] * 4 + [dma((2, ne))] * 3 + [dma((half,))] * 2 + [dma((chunks, half))] * 4
     sems += [dma((chunks, ne))] * 2 + [dma((2 * chunks + 1,))] * 2 + [dma((7,))]
     hbm = pl.BlockSpec(memory_space=pltpu.HBM)
     vmem = pl.BlockSpec(memory_space=pltpu.VMEM)

time: 64.9 us -> 64.5 us (level)
  no operation moved by 1% of the time
where the time goes in v4:
time: 64.5 us; the launch traced here: 64.3 us
  Pallas kernels  62.5 us (97%)
  other arithmetic  1.78 us (3%)
    pallas_call x1, Pallas kernels, shards(): pl.pallas_call(functools.partial(kernel, nv, ne, chunks), out_shape=jax.S...  62.5 us
    convert_element_type x1, other arithmetic, shards(): return pl.pallas_call(functools.partial(kernel, nv, ne, chunks), out_shap...  1.78 us

profile of v4, /device:TPU:0, one launch (start us, length us, event | category | flops | bytes accessed | tf_op | source)
XLA Modules:
  0.0 64.3 jit_solution(9745316228024634372)
XLA Ops:
  0.0 62.5 %shard_map.82 = bf16[512,256]{1,0:T(8,128)(2,1)} custom-call(f32[2048,256]{1,0:T(8,128)} %feat.1, bf16[8,128,128]{2,1,0:T(8,128)(2,1)} %inc.1, s32[1,8]{1,0:T(1,128)} %bitcast.5, s32[1,8]{1,0:T(1,128)} %bitcast.6, s32[1,8]{1,0:T(1,128)} %bitcast.7, f32[2,128]{1,0:T(2,128)} %weight.1, s32[2,128]{1,0:T(2,128)} %degree.1, s32[16,128]{1,0:T(8,128)} %bitcast.4), custom_call_target="tpu_custom_call" | custom-call | flops 268435456 | bytes 2359296 | tf_op jit(solution)/shard_map/pallas_call | solution.py:621
  62.5 1.8 %convert_element_type.3 = f32[512,256]{1,0:T(8,128)} convert(bf16[512,256]{1,0:T(8,128)(2,1)} %shard_map.82) | non-fusion elementwise | flops 131072 | bytes 786432 | tf_op jit(solution)/shard_map/convert_element_type | solution.py:646

commit v5 on v4

--- a/solution.py
+++ b/solution.py
@@ -23,7 +23,6 @@
 def kernel(
     nv,
     ne,
-    chunks,
     feat,
     inc,
     live_s,
@@ -81,9 +80,9 @@
     v = lax.axis_index("vert")
     e = lax.axis_index("edge")
     block = inc.shape[1]
-    blocks = xs.shape[1]
-    part_cols = xs.shape[2]
-    cols = chunks * part_cols
+    blocks = xs.shape[0]
+    cols = xs.shape[1]
+    pairs = ne // 2
     hyper_blocks = weight.shape[0]
     share = blocks // ne
     none = nv * ne
@@ -97,8 +96,8 @@
         first = e + (j % 2) * (sibling - e)
         return (first + 2 * (j // 2)) % ne
 
-    def pair_at(m):
-        return pl.ds((e - e % 2 + 2 * m) % ne, 2)
+    def edge_of(m, pos):
+        return (e - e % 2 + 2 * m) % ne + pos
 
     def ahead(t):
         return base + (here + t) % half
@@ -204,24 +203,17 @@
             for g in range(1, group):
                 picked = jnp.where(part == g, turned[g * cols : (g + 1) * cols], picked)
             picked = (picked * rs[pl.ds(b, 1), :]).astype(BF16)
-            for c in range(chunks):
-                xs[c, b] = picked[c * part_cols : (c + 1) * part_cols]
+            xs[b] = picked
 
     repeat(0, blocks // unit, prepare)
     fetches[4].wait()
 
-    def slot_of(j, s):
-        if j == 0:
-            return live_s[0, s] > 0, row_s[0, s]
-        key = keys[edge_at(j), 0, s]
-        return key >= 0, jnp.maximum(key, 0)
-
-    def partial(j, s, some):
-        alive, row = slot_of(j, s)
-        held = [xs[c, row] for c in some]
-        left = held[0] if len(held) == 1 else jnp.concatenate(held, axis=0)
-        value = jnp.dot(left, tiles[edge_at(j), s], preferred_element_type=F32)
-        return jnp.where(alive, value, 0.0).astype(BF16)
+    def partial(other, s):
+        key = keys[other, 0, s]
+        value = jnp.dot(
+            xs[jnp.maximum(key, 0)], tiles[other, s], preferred_element_type=F32
+        )
+        return jnp.where(key >= 0, value, 0.0).astype(BF16)
 
     def fwd_copy(c, t):
         return to_vert(
@@ -285,40 +277,8 @@
         )
 
     scale_copy = to_vert(
-        scale_e, scale_m, mir_send_sem.at[2 * chunks], mir_recv_sem.at[2 * chunks], mirror
+        scale_e, scale_m, mir_send_sem.at[2 * pairs], mir_recv_sem.at[2 * pairs], mirror
     )
-
-    def first_part(j, q):
-        other = edge_at(j)
-
-        def step(t):
-            value = partial(j, q * half + (here + t) % half, range(chunks))
-            for c in range(chunks):
-                fwd_send[c, t, other, q] = value[c * part_cols : (c + 1) * part_cols]
-
-        repeat(1, half, step)
-        value = partial(j, q * half + here, range(chunks))
-        for c in range(chunks):
-            fwd_recv[c, here, other, q] = value[c * part_cols : (c + 1) * part_cols]
-
-    def first_pair(m):
-        pair = pair_at(m)
-
-        for c in range(chunks):
-
-            def step(t):
-                to_vert(
-                    fwd_send.at[c, t, pair],
-                    fwd_recv.at[c, here, pair],
-                    fwd_send_sem.at[c, t],
-                    fwd_recv_sem.at[c, here],
-                    ahead(t),
-                ).start()
-
-            repeat(1, half, step)
-
-    for q in range(2):
-        first_part(0, q)
 
     for j in range(1, ne):
         source = edge_at(j)
@@ -354,22 +314,106 @@
             copy.start()
             relays.append(copy)
 
+    def send_all(m):
+        def step(t):
+            for pos in range(2):
+                for q in range(2):
+                    slot = q * half + (here + t) % half
+                    fwd_send[m, t, pos, q] = partial(edge_of(m, pos), slot)
+            fwd_copy(m, t).start()
+
+        repeat(1, half, step)
+        for pos in range(2):
+            for q in range(2):
+                fwd_recv[m, here, pos, q] = partial(edge_of(m, pos), q * half + here)
+
+    def sum_half(m, applied):
+        def add_from(source, first):
+            for pos in range(2):
+                for q in range(2):
+                    held = owner_blocks[source, edge_of(m, pos), q * half + here]
+                    value = fwd_recv[m, source, pos, q].astype(F32)
+                    for h in range(hyper_blocks):
+                        term = jnp.where(held == h, value, 0.0)
+                        if not first:
+                            term = hyper_acc[m, q, h, pos] + term
+                        hyper_acc[m, q, h, pos] = term
+
+        add_from(here, True)
+
+        def arrive(t):
+            fwd_arrival(m, behind(t)).wait_recv()
+            add_from(behind(t), False)
+
+        repeat(1, half, arrive)
+        mir_send[applied * pairs + m] = hyper_acc[m].astype(BF16)
+        mir_copy(applied * pairs + m).start()
+        repeat(1, half, lambda t: fwd_copy(m, t).wait_send())
+
+    def answer_all(m, applied):
+        p = applied * pairs + m
+        mir_copy(p).wait_recv()
+        for q in range(2):
+            own = q == v // half
+            for pos in range(2):
+                other = edge_of(m, pos)
+                scale = jnp.where(own, scale_e[other], scale_m[other])
+                for h in range(hyper_blocks):
+                    total = hyper_acc[m, q, h, pos] + mir_recv[p, q, h, pos].astype(F32)
+                    hyper_feat[q, h, pos] = (total * scale[h : h + 1, :]).astype(BF16)
+
+        def answer(t):
+            if applied:
+                bwd_copy(m, t).wait_send()
+            for pos in range(2):
+                for q in range(2):
+                    held = owner_blocks[(here + t) % half, edge_of(m, pos), q * half + here]
+                    bwd_send[m, t, pos, q] = hyper_feat[q, held, pos]
+            bwd_copy(m, t).start()
+
+        repeat(1, half, answer)
+        for pos in range(2):
+            for q in range(2):
+                held = owner_blocks[here, edge_of(m, pos), q * half + here]
+                bwd_recv[m, here, pos, q] = hyper_feat[q, held, pos]
+
+    def gather_rows(m):
+        def spread(t):
+            values = [
+                lax.dot_general(
+                    bwd_recv[m, behind(t), pos, q],
+                    tiles[edge_of(m, pos), q * half + behind(t)],
+                    (((1,), (1,)), ((), ())),
+                    preferred_element_type=F32,
+                )
+                for q in range(2)
+                for pos in range(2)
+            ]
+            for n, value in enumerate(values):
+                i = (m * half + t) * 4 + n
+                acc[i] = value + acc[prev[i]]
+
+        spread(0)
+
+        def come_back(t):
+            bwd_arrival(m, behind(t)).wait_recv()
+            spread(t)
+
+        repeat(1, half, come_back)
+
+    def scale_again(u):
+        for i in range(unit):
+            b = u * unit + i
+            scale = rs[pl.ds(b, 1), :]
+            xs[b] = (scale * (scale * acc[last[b]])).astype(BF16)
+
     for q in range(2):
         relay(1, q)
-        first_part(1, q)
-    first_pair(0)
-    for m in range(1, ne // 2):
-        for q in range(2):
-            relay(2 * m, q)
-            first_part(2 * m, q)
-        for q in range(2):
-            relay(2 * m + 1, q)
-            first_part(2 * m + 1, q)
-        first_pair(m)
-
+    send_all(0)
     def link(i, latest):
-        slot = ((i // ne) % 2) * half + behind(i // (2 * ne))
-        key = keys[edge_at(i % ne), 0, slot]
+        other = edge_of(i // (4 * half), i % 2)
+        slot = ((i // 2) % 2) * half + behind((i // 4) % half)
+        key = keys[other, 0, slot]
         before = none
         for b in range(blocks):
             before = jnp.where(key == b, latest[b], before)
@@ -379,169 +423,63 @@
     latest = lax.fori_loop(0, none, link, (jnp.int32(none),) * blocks)
     for b in range(blocks):
         last[b] = latest[b]
-    for c in range(chunks):
-        acc[c, none] = jnp.zeros(acc.shape[2:], F32)
+    acc[none] = jnp.zeros(acc.shape[1:], F32)
 
     repeat(1, half, lambda t: mv_arrival(behind(t)).wait_recv())
     to_scalars = pltpu.make_async_copy(meta_v, owner_blocks, local_sem.at[1])
     to_scalars.start()
     to_scalars.wait()
 
-    def send_again(c):
-        def send_all(t):
-            for j in range(ne):
-                for q in range(2):
-                    slot = q * half + (here + t) % half
-                    fwd_send[c, t, edge_at(j), q] = partial(j, slot, (c,))
-            fwd_copy(c, t).start()
-
-        repeat(1, half, send_all)
-        for j in range(ne):
-            for q in range(2):
-                fwd_recv[c, here, edge_at(j), q] = partial(j, q * half + here, (c,))
-
-    def sum_half(c, applied):
-        def add_from(source, first):
-            for other in range(ne):
-                for q in range(2):
-                    held = owner_blocks[source, other, q * half + here]
-                    value = fwd_recv[c, source, other, q].astype(F32)
-                    for h in range(hyper_blocks):
-                        term = jnp.where(held == h, value, 0.0)
-                        if not first:
-                            term = hyper_acc[c, q, h, other] + term
-                        hyper_acc[c, q, h, other] = term
-
-        add_from(here, True)
-
-        def arrive(t):
-            fwd_arrival(c, behind(t)).wait_recv()
-            add_from(behind(t), False)
-
-        repeat(1, half, arrive)
-        mir_send[applied * chunks + c] = hyper_acc[c].astype(BF16)
-        mir_copy(applied * chunks + c).start()
-        repeat(1, half, lambda t: fwd_copy(c, t).wait_send())
-
-    def answer_all(c, applied):
-        mir_copy(applied * chunks + c).wait_recv()
+    for m in range(1, pairs):
         for q in range(2):
-            own = q == v // half
-            for other in range(ne):
-                scale = jnp.where(own, scale_e[other], scale_m[other])
-                for h in range(hyper_blocks):
-                    total = hyper_acc[c, q, h, other] + mir_recv[
-                        applied * chunks + c, q, h, other
-                    ].astype(F32)
-                    hyper_feat[q, h, other] = (total * scale[h : h + 1, :]).astype(BF16)
-
-        def answer(t):
-            @pl.when(applied > 0)
-            def _():
-                bwd_copy(c, t).wait_send()
-
-            for other in range(ne):
-                for q in range(2):
-                    held = owner_blocks[(here + t) % half, other, q * half + here]
-                    bwd_send[c, t, other, q] = hyper_feat[q, held, other]
-            bwd_copy(c, t).start()
-
-        repeat(1, half, answer)
-        for other in range(ne):
-            for q in range(2):
-                held = owner_blocks[here, other, q * half + here]
-                bwd_recv[c, here, other, q] = hyper_feat[q, held, other]
-
-    def gather_rows(c):
-        def spread(t):
-            for q in range(2):
-                for j in range(ne):
-                    i = t * 2 * ne + q * ne + j
-                    value = lax.dot_general(
-                        bwd_recv[c, behind(t), edge_at(j), q],
-                        tiles[edge_at(j), q * half + behind(t)],
-                        (((1,), (1,)), ((), ())),
-                        preferred_element_type=F32,
-                    )
-                    acc[c, i] = value + acc[c, prev[i]]
-
-        spread(0)
-
-        def come_back(t):
-            bwd_arrival(c, behind(t)).wait_recv()
-            spread(t)
-
-        repeat(1, half, come_back)
-
-    def fin_copy(c, j):
+            relay(2 * m, q)
+    sum_half(0, 0)
+    for m in range(1, pairs):
+        for q in range(2):
+            relay(2 * m + 1, q)
+        send_all(m)
+        sum_half(m, 0)
+    scale_copy.wait_recv()
+
+    for applied in range(2):
+        if applied:
+            for m in range(pairs):
+                send_all(m)
+            for m in range(pairs):
+                sum_half(m, 1)
+        for m in range(pairs):
+            answer_all(m, applied)
+        for m in range(pairs):
+            gather_rows(m)
+        if not applied:
+            repeat(0, blocks // unit, scale_again)
+
+    def fin_copy(j):
         return to_edge(
-            fin_send.at[c, j],
-            fin_recv.at[c, e],
-            fin_send_sem.at[c, j],
-            fin_recv_sem.at[c, e],
-            edge_at(j),
-        )
-
-    def finish(c):
-        for j in range(ne - 1, -1, -1):
-            for k in range(share):
-                b = edge_at(j) * share + k
-                value = (rs[pl.ds(b, 1), :] * acc[c, last[b]]).astype(BF16)
-                if j:
-                    fin_send[c, j, k] = value
-                else:
-                    fin_recv[c, e, k] = value
+            fin_send.at[j], fin_recv.at[e], fin_send_sem.at[j], fin_recv_sem.at[e], edge_at(j)
+        )
+
+    for j in range(ne - 1, -1, -1):
+        for k in range(share):
+            b = edge_at(j) * share + k
+            value = (rs[pl.ds(b, 1), :] * acc[last[b]]).astype(BF16)
             if j:
-                fin_copy(c, j).start()
-
-    def scale_again(c):
-        def rescale(u):
-            for i in range(unit):
-                b = u * unit + i
-                scale = rs[pl.ds(b, 1), :]
-                xs[c, b] = (scale * (scale * acc[c, last[b]])).astype(BF16)
-
-        repeat(0, blocks // unit, rescale)
-
-    scale_copy.wait_recv()
-
-    def one_pass(applied):
-        repeat(0, chunks, lambda c: sum_half(c, applied))
-        repeat(0, chunks, lambda c: answer_all(c, applied))
-
-        def rows(c):
-            gather_rows(c)
-
-            @pl.when(applied == 0)
-            def _():
-                scale_again(c)
-                send_again(c)
-
-            @pl.when(applied > 0)
-            def _():
-                finish(c)
-
-        repeat(0, chunks, rows)
-
-    repeat(0, 2, one_pass)
-
-    for c in range(chunks):
-        for j in range(1, ne):
-            source = edge_at(j)
-            to_edge(
-                fin_send.at[c, 0],
-                fin_recv.at[c, source],
-                fin_send_sem.at[c, 0],
-                fin_recv_sem.at[c, source],
-                e,
-            ).wait_recv()
+                fin_send[j, k] = value
+            else:
+                fin_recv[e, k] = value
+        if j:
+            fin_copy(j).start()
+    for j in range(1, ne):
+        source = edge_at(j)
+        to_edge(
+            fin_send.at[0], fin_recv.at[source], fin_send_sem.at[0], fin_recv_sem.at[source], e
+        ).wait_recv()
     for k in range(share):
         for g in range(ne // group):
             stacked = jnp.concatenate(
                 [
-                    fin_recv[c, g * group + i, k].astype(F32)
+                    fin_recv[g * group + i, k].astype(F32)
                     for i in range(group)
-                    for c in range(chunks)
                 ],
                 axis=0,
             )
@@ -551,12 +489,12 @@
         copy.wait_send()
     repeat(1, half, lambda t: mv_copy(t).wait_send())
     scale_copy.wait_send()
-    for c in range(chunks):
+    for m in range(pairs):
         for applied in range(2):
-            mir_copy(applied * chunks + c).wait_send()
-        repeat(1, half, lambda t: bwd_copy(c, t).wait_send())
-        for j in range(1, ne):
-            fin_copy(c, j).wait_send()
+            mir_copy(applied * pairs + m).wait_send()
+        repeat(1, half, lambda t: bwd_copy(m, t).wait_send())
+    for j in range(1, ne):
+        fin_copy(j).wait_send()
 
 
 def shards(
@@ -571,8 +509,7 @@
     cols = width // ne
     share = blocks // ne
     half = nv // 2
-    chunks = max(1, cols // 32)
-    cut = cols // chunks
+    pairs = ne // 2
     scratch = [
         ((papers, LANES), F32),
         ((hyper_blocks, block), F32),
@@ -585,21 +522,21 @@
         ((half, 8, LANES), jnp.int32),
         None,
         None,
-        ((chunks, blocks, cut, block), BF16),
+        ((blocks, cols, block), BF16),
         ((blocks, block), F32),
-        ((chunks, half, ne, 2, cut, block), BF16),
-        ((chunks, half, ne, 2, cut, block), BF16),
-        ((chunks, half, ne, 2, cut, block), BF16),
-        ((chunks, half, ne, 2, cut, block), BF16),
-        ((chunks, nv * ne + 1, cut, block), F32),
+        ((pairs, half, 2, 2, cols, block), BF16),
+        ((pairs, half, 2, 2, cols, block), BF16),
+        ((pairs, half, 2, 2, cols, block), BF16),
+        ((pairs, half, 2, 2, cols, block), BF16),
+        ((nv * ne + 1, cols, block), F32),
         None,
         None,
-        ((chunks, 2, hyper_blocks, ne, cut, block), F32),
-        ((2, hyper_blocks, ne, cut, block), BF16),
-        ((2 * chunks, 2, hyper_blocks, ne, cut, block), BF16),
-        ((2 * chunks, 2, hyper_blocks, ne, cut, block), BF16),
-        ((chunks, ne, share, cut, block), BF16),
-        ((chunks, ne, share, cut, block), BF16),
+        ((pairs, 2, hyper_blocks, 2, cols, block), F32),
+        ((2, hyper_blocks, 2, cols, block), BF16),
+        ((2 * pairs, 2, hyper_blocks, 2, cols, block), BF16),
+        ((2 * pairs, 2, hyper_blocks, 2, cols, block), BF16),
+        ((ne, share, cols, block), BF16),
+        ((ne, share, cols, block), BF16),
     ]
     scalars = iter(
         [(ne, 8, LANES), (half, 8, LANES), (nv * ne,), (blocks,)]
@@ -613,13 +550,13 @@
         for item in scratch
     ]
     dma = pltpu.SemaphoreType.DMA
-    sems = [dma((ne,))] * 4 + [dma((2, ne))] * 3 + [dma((half,))] * 2 + [dma((chunks, half))] * 4
-    sems += [dma((chunks, ne))] * 2 + [dma((2 * chunks + 1,))] * 2 + [dma((7,))]
+    sems = [dma((ne,))] * 4 + [dma((2, ne))] * 3 + [dma((half,))] * 2 + [dma((pairs, half))] * 4
+    sems += [dma((ne,))] * 2 + [dma((2 * pairs + 1,))] * 2 + [dma((7,))]
     hbm = pl.BlockSpec(memory_space=pltpu.HBM)
     vmem = pl.BlockSpec(memory_space=pltpu.VMEM)
     smem = pl.BlockSpec(memory_space=pltpu.SMEM)
     return pl.pallas_call(
-        functools.partial(kernel, nv, ne, chunks),
+        functools.partial(kernel, nv, ne),
         out_shape=jax.ShapeDtypeStruct((papers // ne, width), BF16),
         in_specs=[hbm, hbm, smem, smem, smem, hbm, hbm, hbm],
         out_specs=vmem,

time: 64.5 us -> 63.4 us (0.983)
  Pallas kernels: 62.5 us -> 61.4 us
    pallas_call x1, Pallas kernels: 62.5 us -> 61.4 us  [shards(): pl.pallas_call(functools.partial(kernel, nv, ne), out_shape=jax.ShapeDtyp...]
where the time goes in v5:
time: 63.4 us; the launch traced here: 63.2 us
  Pallas kernels  61.4 us (97%)
  other arithmetic  1.78 us (3%)
    pallas_call x1, Pallas kernels, shards(): pl.pallas_call(functools.partial(kernel, nv, ne), out_shape=jax.ShapeDtyp...  61.4 us
    convert_element_type x1, other arithmetic, shards(): return pl.pallas_call(functools.partial(kernel, nv, ne), out_shape=jax.Sh...  1.78 us

profile of v5, /device:TPU:0, one launch (start us, length us, event | category | flops | bytes accessed | tf_op | source)
XLA Modules:
  0.0 63.2 jit_solution(12161384325556632172)
XLA Ops:
  0.0 61.4 %shard_map.82 = bf16[512,256]{1,0:T(8,128)(2,1)} custom-call(f32[2048,256]{1,0:T(8,128)} %feat.1, bf16[8,128,128]{2,1,0:T(8,128)(2,1)} %inc.1, s32[1,8]{1,0:T(1,128)} %bitcast.5, s32[1,8]{1,0:T(1,128)} %bitcast.6, s32[1,8]{1,0:T(1,128)} %bitcast.7, f32[2,128]{1,0:T(2,128)} %weight.1, s32[2,128]{1,0:T(2,128)} %degree.1, s32[16,128]{1,0:T(8,128)} %bitcast.4), custom_call_target="tpu_custom_call" | custom-call | flops 268435456 | bytes 2359296 | tf_op jit(solution)/shard_map/pallas_call | solution.py:558
  61.5 1.8 %convert_element_type.3 = f32[512,256]{1,0:T(8,128)} convert(bf16[512,256]{1,0:T(8,128)(2,1)} %shard_map.82) | non-fusion elementwise | flops 131072 | bytes 786432 | tf_op jit(solution)/shard_map/convert_element_type | solution.py:583

commit v6 on v5

--- a/solution.py
+++ b/solution.py
@@ -82,7 +82,6 @@
     block = inc.shape[1]
     blocks = xs.shape[0]
     cols = xs.shape[1]
-    pairs = ne // 2
     hyper_blocks = weight.shape[0]
     share = blocks // ne
     none = nv * ne
@@ -95,9 +94,6 @@
     def edge_at(j):
         first = e + (j % 2) * (sibling - e)
         return (first + 2 * (j // 2)) % ne
-
-    def edge_of(m, pos):
-        return (e - e % 2 + 2 * m) % ne + pos
 
     def ahead(t):
         return base + (here + t) % half
@@ -277,7 +273,7 @@
         )
 
     scale_copy = to_vert(
-        scale_e, scale_m, mir_send_sem.at[2 * pairs], mir_recv_sem.at[2 * pairs], mirror
+        scale_e, scale_m, mir_send_sem.at[2 * ne], mir_recv_sem.at[2 * ne], mirror
     )
 
     for j in range(1, ne):
@@ -314,30 +310,28 @@
             copy.start()
             relays.append(copy)
 
-    def send_all(m):
+    def send_all(m, again=False):
         def step(t):
-            for pos in range(2):
-                for q in range(2):
-                    slot = q * half + (here + t) % half
-                    fwd_send[m, t, pos, q] = partial(edge_of(m, pos), slot)
+            if again:
+                fwd_copy(m, t).wait_send()
+            for q in range(2):
+                fwd_send[m, t, q] = partial(edge_at(m), q * half + (here + t) % half)
             fwd_copy(m, t).start()
 
         repeat(1, half, step)
-        for pos in range(2):
-            for q in range(2):
-                fwd_recv[m, here, pos, q] = partial(edge_of(m, pos), q * half + here)
+        for q in range(2):
+            fwd_recv[m, here, q] = partial(edge_at(m), q * half + here)
 
     def sum_half(m, applied):
         def add_from(source, first):
-            for pos in range(2):
-                for q in range(2):
-                    held = owner_blocks[source, edge_of(m, pos), q * half + here]
-                    value = fwd_recv[m, source, pos, q].astype(F32)
-                    for h in range(hyper_blocks):
-                        term = jnp.where(held == h, value, 0.0)
-                        if not first:
-                            term = hyper_acc[m, q, h, pos] + term
-                        hyper_acc[m, q, h, pos] = term
+            for q in range(2):
+                held = owner_blocks[source, edge_at(m), q * half + here]
+                value = fwd_recv[m, source, q].astype(F32)
+                for h in range(hyper_blocks):
+                    term = jnp.where(held == h, value, 0.0)
+                    if not first:
+                        term = hyper_acc[m, q, h] + term
+                    hyper_acc[m, q, h] = term
 
         add_from(here, True)
 
@@ -346,51 +340,45 @@
             add_from(behind(t), False)
 
         repeat(1, half, arrive)
-        mir_send[applied * pairs + m] = hyper_acc[m].astype(BF16)
-        mir_copy(applied * pairs + m).start()
-        repeat(1, half, lambda t: fwd_copy(m, t).wait_send())
+        mir_send[applied * ne + m] = hyper_acc[m].astype(BF16)
+        mir_copy(applied * ne + m).start()
 
     def answer_all(m, applied):
-        p = applied * pairs + m
+        p = applied * ne + m
         mir_copy(p).wait_recv()
         for q in range(2):
             own = q == v // half
-            for pos in range(2):
-                other = edge_of(m, pos)
-                scale = jnp.where(own, scale_e[other], scale_m[other])
-                for h in range(hyper_blocks):
-                    total = hyper_acc[m, q, h, pos] + mir_recv[p, q, h, pos].astype(F32)
-                    hyper_feat[q, h, pos] = (total * scale[h : h + 1, :]).astype(BF16)
+            scale = jnp.where(own, scale_e[edge_at(m)], scale_m[edge_at(m)])
+            for h in range(hyper_blocks):
+                total = hyper_acc[m, q, h] + mir_recv[p, q, h].astype(F32)
+                hyper_feat[q, h] = (total * scale[h : h + 1, :]).astype(BF16)
 
         def answer(t):
             if applied:
                 bwd_copy(m, t).wait_send()
-            for pos in range(2):
-                for q in range(2):
-                    held = owner_blocks[(here + t) % half, edge_of(m, pos), q * half + here]
-                    bwd_send[m, t, pos, q] = hyper_feat[q, held, pos]
+            for q in range(2):
+                held = owner_blocks[(here + t) % half, edge_at(m), q * half + here]
+                bwd_send[m, t, q] = hyper_feat[q, held]
             bwd_copy(m, t).start()
 
         repeat(1, half, answer)
-        for pos in range(2):
-            for q in range(2):
-                held = owner_blocks[here, edge_of(m, pos), q * half + here]
-                bwd_recv[m, here, pos, q] = hyper_feat[q, held, pos]
+        for q in range(2):
+            held = owner_blocks[here, edge_at(m), q * half + here]
+            bwd_recv[m, here, q] = hyper_feat[q, held]
 
     def gather_rows(m):
         def spread(t):
             values = [
                 lax.dot_general(
-                    bwd_recv[m, behind(t), pos, q],
-                    tiles[edge_of(m, pos), q * half + behind(t)],
+                    bwd_recv[m, behind(t), q],
+                    tiles[edge_at(m), q * half + behind(t)],
                     (((1,), (1,)), ((), ())),
                     preferred_element_type=F32,
                 )
                 for q in range(2)
-                for pos in range(2)
             ]
             for n, value in enumerate(values):
-                i = (m * half + t) * 4 + n
+                i = (m * half + t) * 2 + n
                 acc[i] = value + acc[prev[i]]
 
         spread(0)
@@ -407,12 +395,13 @@
             scale = rs[pl.ds(b, 1), :]
             xs[b] = (scale * (scale * acc[last[b]])).astype(BF16)
 
+    send_all(0)
     for q in range(2):
         relay(1, q)
-    send_all(0)
+    send_all(1)
     def link(i, latest):
-        other = edge_of(i // (4 * half), i % 2)
-        slot = ((i // 2) % 2) * half + behind((i // 4) % half)
+        other = edge_at(i // (2 * half))
+        slot = (i % 2) * half + behind((i // 2) % half)
         key = keys[other, 0, slot]
         before = none
         for b in range(blocks):
@@ -430,26 +419,24 @@
     to_scalars.start()
     to_scalars.wait()
 
-    for m in range(1, pairs):
+    for m in range(2, ne):
+        sum_half(m - 2, 0)
         for q in range(2):
-            relay(2 * m, q)
-    sum_half(0, 0)
-    for m in range(1, pairs):
-        for q in range(2):
-            relay(2 * m + 1, q)
+            relay(m, q)
         send_all(m)
+    for m in range(ne - 2, ne):
         sum_half(m, 0)
     scale_copy.wait_recv()
 
     for applied in range(2):
         if applied:
-            for m in range(pairs):
-                send_all(m)
-            for m in range(pairs):
+            for m in range(ne):
+                send_all(m, True)
+            for m in range(ne):
                 sum_half(m, 1)
-        for m in range(pairs):
+        for m in range(ne):
             answer_all(m, applied)
-        for m in range(pairs):
+        for m in range(ne):
             gather_rows(m)
         if not applied:
             repeat(0, blocks // unit, scale_again)
@@ -489,9 +476,10 @@
         copy.wait_send()
     repeat(1, half, lambda t: mv_copy(t).wait_send())
     scale_copy.wait_send()
-    for m in range(pairs):
+    for m in range(ne):
         for applied in range(2):
-            mir_copy(applied * pairs + m).wait_send()
+            mir_copy(applied * ne + m).wait_send()
+        repeat(1, half, lambda t: fwd_copy(m, t).wait_send())
         repeat(1, half, lambda t: bwd_copy(m, t).wait_send())
     for j in range(1, ne):
         fin_copy(j).wait_send()
@@ -509,7 +497,6 @@
     cols = width // ne
     share = blocks // ne
     half = nv // 2
-    pairs = ne // 2
     scratch = [
         ((papers, LANES), F32),
         ((hyper_blocks, block), F32),
@@ -524,17 +511,17 @@
         None,
         ((blocks, cols, block), BF16),
         ((blocks, block), F32),
-        ((pairs, half, 2, 2, cols, block), BF16),
-        ((pairs, half, 2, 2, cols, block), BF16),
-        ((pairs, half, 2, 2, cols, block), BF16),
-        ((pairs, half, 2, 2, cols, block), BF16),
+        ((ne, half, 2, cols, block), BF16),
+        ((ne, half, 2, cols, block), BF16),
+        ((ne, half, 2, cols, block), BF16),
+        ((ne, half, 2, cols, block), BF16),
         ((nv * ne + 1, cols, block), F32),
         None,
         None,
-        ((pairs, 2, hyper_blocks, 2, cols, block), F32),
-        ((2, hyper_blocks, 2, cols, block), BF16),
-        ((2 * pairs, 2, hyper_blocks, 2, cols, block), BF16),
-        ((2 * pairs, 2, hyper_blocks, 2, cols, block), BF16),
+        ((ne, 2, hyper_blocks, cols, block), F32),
+        ((2, hyper_blocks, cols, block), BF16),
+        ((2 * ne, 2, hyper_blocks, cols, block), BF16),
+        ((2 * ne, 2, hyper_blocks, cols, block), BF16),
         ((ne, share, cols, block), BF16),
         ((ne, share, cols, block), BF16),
     ]
@@ -550,8 +537,8 @@
         for item in scratch
     ]
     dma = pltpu.SemaphoreType.DMA
-    sems = [dma((ne,))] * 4 + [dma((2, ne))] * 3 + [dma((half,))] * 2 + [dma((pairs, half))] * 4
-    sems += [dma((ne,))] * 2 + [dma((2 * pairs + 1,))] * 2 + [dma((7,))]
+    sems = [dma((ne,))] * 4 + [dma((2, ne))] * 3 + [dma((half,))] * 2 + [dma((ne, half))] * 4
+    sems += [dma((ne,))] * 2 + [dma((2 * ne + 1,))] * 2 + [dma((7,))]
     hbm = pl.BlockSpec(memory_space=pltpu.HBM)
     vmem = pl.BlockSpec(memory_space=pltpu.VMEM)
     smem = pl.BlockSpec(memory_space=pltpu.SMEM)

time: 63.4 us -> 58.5 us (0.923)
  Pallas kernels: 61.4 us -> 56.5 us
    pallas_call x1, Pallas kernels: 61.4 us -> 56.5 us  [shards(): pl.pallas_call(functools.partial(kernel, nv, ne), out_shape=jax.ShapeDtyp...]
where the time goes in v6:
time: 58.5 us; the launch traced here: 58.3 us
  Pallas kernels  56.5 us (97%)
  other arithmetic  1.78 us (3%)
    pallas_call x1, Pallas kernels, shards(): pl.pallas_call(functools.partial(kernel, nv, ne), out_shape=jax.ShapeDtyp...  56.5 us
    convert_element_type x1, other arithmetic, shards(): return pl.pallas_call(functools.partial(kernel, nv, ne), out_shape=jax.Sh...  1.78 us

profile of v6, /device:TPU:0, one launch (start us, length us, event | category | flops | bytes accessed | tf_op | source)
XLA Modules:
  0.0 58.3 jit_solution(8065886956188461912)
XLA Ops:
  0.0 56.5 %shard_map.82 = bf16[512,256]{1,0:T(8,128)(2,1)} custom-call(f32[2048,256]{1,0:T(8,128)} %feat.1, bf16[8,128,128]{2,1,0:T(8,128)(2,1)} %inc.1, s32[1,8]{1,0:T(1,128)} %bitcast.5, s32[1,8]{1,0:T(1,128)} %bitcast.6, s32[1,8]{1,0:T(1,128)} %bitcast.7, f32[2,128]{1,0:T(2,128)} %weight.1, s32[2,128]{1,0:T(2,128)} %degree.1, s32[16,128]{1,0:T(8,128)} %bitcast.4), custom_call_target="tpu_custom_call" | custom-call | flops 268435456 | bytes 2359296 | tf_op jit(solution)/shard_map/pallas_call | solution.py:545
  56.5 1.8 %convert_element_type.3 = f32[512,256]{1,0:T(8,128)} convert(bf16[512,256]{1,0:T(8,128)(2,1)} %shard_map.82) | non-fusion elementwise | flops 131072 | bytes 786432 | tf_op jit(solution)/shard_map/convert_element_type | solution.py:570

commit v7 on v6

--- a/solution.py
+++ b/solution.py
@@ -15,9 +15,14 @@
 
 
 def repeat(start, stop, body):
-    @pl.loop(start, stop)
-    def _(step):
-        body(step)
+    if stop - start <= 3:
+        for step in range(start, stop):
+            body(step)
+    else:
+
+        @pl.loop(start, stop)
+        def _(step):
+            body(step)
 
 
 def kernel(
@@ -436,7 +441,9 @@
                 sum_half(m, 1)
         for m in range(ne):
             answer_all(m, applied)
-        for m in range(ne):
+            if m >= 2:
+                gather_rows(m - 2)
+        for m in range(ne - 2, ne):
             gather_rows(m)
         if not applied:
             repeat(0, blocks // unit, scale_again)

time: 58.5 us -> 60.4 us (1.032)
  Pallas kernels: 56.5 us -> 58.4 us
    pallas_call x1, Pallas kernels: 56.5 us -> 58.4 us  [shards(): pl.pallas_call(functools.partial(kernel, nv, ne), out_shape=jax.ShapeDtyp...]
where the time goes in v7:
time: 60.4 us; the launch traced here: 60.2 us
  Pallas kernels  58.4 us (97%)
  other arithmetic  1.78 us (3%)
    pallas_call x1, Pallas kernels, shards(): pl.pallas_call(functools.partial(kernel, nv, ne), out_shape=jax.ShapeDtyp...  58.4 us
    convert_element_type x1, other arithmetic, shards(): return pl.pallas_call(functools.partial(kernel, nv, ne), out_shape=jax.Sh...  1.78 us

profile of v7, /device:TPU:0, one launch (start us, length us, event | category | flops | bytes accessed | tf_op | source)
XLA Modules:
  0.0 60.2 jit_solution(1019349843060321477)
XLA Ops:
  0.0 58.4 %shard_map.82 = bf16[512,256]{1,0:T(8,128)(2,1)} custom-call(f32[2048,256]{1,0:T(8,128)} %feat.1, bf16[8,128,128]{2,1,0:T(8,128)(2,1)} %inc.1, s32[1,8]{1,0:T(1,128)} %bitcast.5, s32[1,8]{1,0:T(1,128)} %bitcast.6, s32[1,8]{1,0:T(1,128)} %bitcast.7, f32[2,128]{1,0:T(2,128)} %weight.1, s32[2,128]{1,0:T(2,128)} %degree.1, s32[16,128]{1,0:T(8,128)} %bitcast.4), custom_call_target="tpu_custom_call" | custom-call | flops 268435456 | bytes 2359296 | tf_op jit(solution)/shard_map/pallas_call | solution.py:552
  58.4 1.8 %convert_element_type.3 = f32[512,256]{1,0:T(8,128)} convert(bf16[512,256]{1,0:T(8,128)(2,1)} %shard_map.82) | non-fusion elementwise | flops 131072 | bytes 786432 | tf_op jit(solution)/shard_map/convert_element_type | solution.py:577
